TPU v7x, 32 devices: a whole 2x2x4 slice. The times are simulated.
32 devices in a mesh: grp: 4 (over y, core), mem: 8 (over z, x).
Axes of the slice: x: 2, y: 2, z: 4, core: 2. Of those that a mesh axis runs over, the one named last changes fastest.
Arguments:
- iterate: bfloat16 [4, 2048, 7168], P(None, ('grp', 'mem')), may hold values from -0.5 to 0.5
- slot_of: int32 [4], replicated, may hold values from 0 to 3, each once
Outputs:
- update: bfloat16 [4, 2048, 7168], P(None, ('grp', 'mem'))
Inputs may be any that keep to these rules, and one draw needn't show every extreme that they name: `slot_of`: each matrix sits in a different slot.
All inputs are finite; a program needn't handle non-finite values.
Results may differ from a plain program's by a relative error of at most 0.038.
Values may be sent and summed in bfloat16 or wider, within the bound.
No kernel may reach another device: no remote copies, remote signals or barrier semaphores. Data moves between devices by JAX's collectives and lax.ppermute only.
A program may use at most 128 MiB of HBM per device.

v0:
```python
import math

import jax
import jax.numpy as jnp
from jax import lax
from jax.sharding import PartitionSpec as P

ITERS = 2


linear_weight = 3.4445
cubic_weight = -4.775
quintic_weight = 2.0315
epsilon = 1e-07


def gram_matrix(current):
    owned_rows = lax.psum_scatter(
        lax.dot_general(
            current, current, (((1,), (1,)), ((), ())), preferred_element_type=jnp.float32
        ).astype(jnp.bfloat16),
        "mem",
        scatter_dimension=0,
        tiled=True,
    )
    return lax.all_gather(owned_rows, "mem", axis=0, tiled=True)


def newton_iteration(current):
    gram = gram_matrix(current)
    product = jnp.dot(gram, current, preferred_element_type=jnp.float32).astype(jnp.bfloat16)
    second = jnp.dot(gram, product, preferred_element_type=jnp.float32)
    mixed = (
        linear_weight * current.astype(jnp.float32)
        + cubic_weight * product.astype(jnp.float32)
        + quintic_weight * second
    )
    return mixed.astype(jnp.bfloat16)


def on_device(iterate, slot_of):
    group_count = lax.axis_size("grp")
    member_count = lax.axis_size("mem")
    mat_count, local_rows, col_count = iterate.shape
    col_width = col_count // member_count
    ordered = jnp.take(iterate, slot_of, axis=0)
    pieces = ordered.reshape(mat_count, local_rows, member_count, col_width).transpose(0, 2, 1, 3)
    arrived = lax.all_to_all(
        pieces.reshape(mat_count * member_count, 1, local_rows, col_width),
        ("grp", "mem"),
        split_axis=0,
        concat_axis=1,
        tiled=True,
    )
    current = arrived.reshape(-1, col_width)
    row_count = current.shape[0]
    for iteration in range(ITERS):
        current = newton_iteration(current)
    target = math.sqrt(row_count * col_count)
    values = current.astype(jnp.float32)
    sum_total = lax.psum(jnp.sum(values * values), "mem")
    leaving = (values * (target / (jnp.sqrt(sum_total) + epsilon))).astype(jnp.bfloat16)
    returned = lax.all_to_all(
        leaving.reshape(group_count * member_count, 1, local_rows, col_width),
        ("grp", "mem"),
        split_axis=0,
        concat_axis=1,
        tiled=True,
    )
    gathered_back = (
        returned.reshape(mat_count, member_count, local_rows, col_width)
        .transpose(0, 2, 1, 3)
        .reshape(mat_count, local_rows, col_count)
    )
    return gathered_back


def solution(mesh):
    return jax.shard_map(
        on_device,
        mesh=mesh,
        in_specs=(P(None, ("grp", "mem"), None), P()),
        out_specs=P(None, ("grp", "mem"), None),
        check_vma=False,
    )
```

profile of v0, /device:TPU:0, one launch (start us, length us, event | category | flops | bytes accessed | tf_op | source)
XLA Modules:
  0.0 841.9 jit_solution(1388696611810391877)
XLA Ops:
  6.5 0.0 reduce-scatter.3.cloned.1.call-start
  6.5 0.7 compare_and_fusion
  7.2 0.7 compare_select_fusion
  7.9 4.7 gather_fusion
  12.5 2.5 bitcast_select_fusion
  15.0 90.9 %all_to_all.8 = bf16[32,1,64,896]{3,2,1,0:T(8,128)(2,1)S(1)} all-to-all(bf16[32,1,64,896]{3,2,1,0:T(8,128)(2,1)S(1)} %bitcast.28), channel_id=1, replica_groups=mesh['grp'=4,'mem'=8] {'grp','mem'}, dimensions={0} | all-to-all | bytes 7340032 | tf_op jit(solution)/shard_map/all_to_all | solution.py:48
  105.9 1.8 copy-done
  107.7 10.9 %convolution_convert_fusion.1 = bf16[2048,2048]{1,0:T(8,128)(2,1)} fusion(bf16[2048,896]{1,0:T(8,128)(2,1)S(1)} %bitcast.31), kind=kOutput, calls=%fused_computation.4 | convolution fusion | flops 7520387072 | bytes 12058624 | tf_op jit(solution)/shard_map/dot_general | solution.py:19
  118.7 0.0 reduce-scatter.3.cloned.1.call-update
  118.7 0.0 all-gather.3.cloned.1.call-start
  118.7 146.8 %reduce-scatter.3.cloned.1.call-done = bf16[256,2048]{1,0:T(8,128)(2,1)} async-done(((bf16[2048,2048]{1,0:T(8,128)(2,1)}), bf16[256,2048]{1,0:T(8,128)(2,1)}) %reduce-scatter.3.cloned.1.call-update) | async-done | bytes 1048592 | tf_op jit(solution)/shard_map/reduce_scatter | solution.py:18
  265.5 0.0 all-gather.3.cloned.1.call-update
  265.5 0.0 reduce-scatter.5.cloned.1.call-start
  265.6 126.2 %all-gather.3.cloned.1.call-done = bf16[2048,2048]{1,0:T(8,128)(2,1)} async-done(((bf16[256,2048]{1,0:T(8,128)(2,1)}), bf16[2048,2048]{1,0:T(8,128)(2,1)}) %all-gather.3.cloned.1.call-update) | async-done | bytes 8388624 | tf_op jit(solution)/shard_map/all_gather | solution.py:26
  391.8 13.3 %fusion.4 = bf16[2048,896]{1,0:T(8,128)(2,1)S(1)} fusion(bf16[2048,2048]{1,0:T(8,128)(2,1)} %all-gather.3.cloned.1.call-done, bf16[2048,896]{1,0:T(8,128)(2,1)} %bitcast.32), kind=kOutput, calls=%fused_computation.15 | convolution fusion | flops 7516192768 | bytes 15728640 | tf_op jit(solution)/shard_map/dot_general | solution.py:31
  405.1 9.3 %add_convert_fusion.1 = bf16[2048,896]{1,0:T(8,128)(2,1)S(1)} fusion(bf16[2048,896]{1,0:T(8,128)(2,1)S(1)} %bitcast.33, bf16[2048,2048]{1,0:T(8,128)(2,1)S(1)} %copy-done.2, bf16[2048,896]{1,0:T(8,128)(2,1)S(1)} %fusion.4), kind=kOutput, calls=%fused_computation.8 | convolution fusion | flops 7530872832 | bytes 19398656 | tf_op jit(solution)/shard_map/dot_general | solution.py:32
  414.5 0.0 copy-start.4
  414.5 1.8 copy-done.4
  416.3 10.9 %convolution_convert_fusion = bf16[2048,2048]{1,0:T(8,128)(2,1)} fusion(bf16[2048,896]{1,0:T(8,128)(2,1)S(1)} %add_convert_fusion.1), kind=kOutput, calls=%fused_computation.3 | convolution fusion | flops 7520387072 | bytes 12058624 | tf_op jit(solution)/shard_map/dot_general | solution.py:19
  427.3 0.0 reduce-scatter.5.cloned.1.call-update
  427.3 0.2 all-gather.5.cloned.1.call-start
  427.5 147.2 %reduce-scatter.5.cloned.1.call-done = bf16[256,2048]{1,0:T(8,128)(2,1)} async-done(((bf16[2048,2048]{1,0:T(8,128)(2,1)}), bf16[256,2048]{1,0:T(8,128)(2,1)}) %reduce-scatter.5.cloned.1.call-update) | async-done | bytes 1048592 | tf_op jit(solution)/shard_map/reduce_scatter | solution.py:18
  574.7 0.0 all-gather.5.cloned.1.call-update
  574.7 125.9 %all-gather.5.cloned.1.call-done = bf16[2048,2048]{1,0:T(8,128)(2,1)} async-done(((bf16[256,2048]{1,0:T(8,128)(2,1)}), bf16[2048,2048]{1,0:T(8,128)(2,1)}) %all-gather.5.cloned.1.call-update) | async-done | bytes 8388624 | tf_op jit(solution)/shard_map/all_gather | solution.py:26
  700.6 12.4 %fusion.5 = bf16[2048,896]{1,0:T(8,128)(2,1)S(1)} fusion(bf16[2048,2048]{1,0:T(8,128)(2,1)} %all-gather.5.cloned.1.call-done, bf16[2048,896]{1,0:T(8,128)(2,1)} %copy-done.4), kind=kOutput, calls=%fused_computation.16 | convolution fusion | flops 7516192768 | bytes 15728640 | tf_op jit(solution)/shard_map/dot_general | solution.py:31
  713.1 0.0 copy-done.3
  713.1 0.0 copy-done.5
  713.1 11.7 %fusion = (f32[]{:T(128)}, bf16[2048,896]{1,0:T(8,128)(2,1)}) fusion(bf16[2048,2048]{1,0:T(8,128)(2,1)S(1)} %copy-done.3, bf16[2048,896]{1,0:T(8,128)(2,1)S(1)} %fusion.5, bf16[2048,896]{1,0:T(8,128)(2,1)S(1)} %copy-done.5), kind=kOutput, calls=%fused_computation.5 | convolution fusion | flops 7536377856 | bytes 19398660 | tf_op jit(solution)/shard_map/dot_general | solution.py:32
  724.8 19.1 %psum.7 = f32[]{:T(128)} all-reduce(f32[]{:T(128)} %get-tuple-element.5), channel_id=1, replica_groups=mesh['grp'=4,'mem'=8] {'mem'}, use_global_device_ids=true, to_apply=%region_3.4 | all-reduce | flops 1 | bytes 8 | tf_op jit(solution)/shard_map/psum | solution.py:61
  744.7 2.7 fusion.1
  747.4 85.6 %all_to_all.9 = bf16[32,1,64,896]{3,2,1,0:T(8,128)(2,1)S(1)} all-to-all(bf16[32,1,64,896]{3,2,1,0:T(8,128)(2,1)S(1)} %bitcast.29), channel_id=1, replica_groups=mesh['grp'=4,'mem'=8] {'grp','mem'}, dimensions={0} | all-to-all | bytes 7340032 | tf_op jit(solution)/shard_map/all_to_all | solution.py:63
  833.0 2.4 copy.9
  (8 shorter events, 0.0 us)
Async XLA Ops:
  6.5 259.0 %reduce-scatter.3.cloned.1.call-start = ((), (), s32[]{:S(2)}) async-start(), calls=%async_computation.4 | async-start | bytes 9437184 | tf_op jit(solution)/shard_map/reduce_scatter | solution.py:18
  105.9 1.8 copy-start
  118.7 273.1 %all-gather.3.cloned.1.call-start = ((), (), s32[]{:S(2)}) async-start(), calls=%async_computation.5 | async-start | bytes 9437184 | tf_op jit(solution)/shard_map/all_gather | solution.py:26
  265.5 309.2 %reduce-scatter.5.cloned.1.call-start = ((), (), s32[]{:S(2)}) async-start(), calls=%async_computation.6 | async-start | bytes 9437184 | tf_op jit(solution)/shard_map/reduce_scatter | solution.py:18
  391.8 13.3 %copy-start.1 = (bf16[32,1,64,896]{3,2,1,0:T(8,128)(2,1)S(1)}, bf16[32,1,64,896]{3,2,1,0:T(8,128)(2,1)}, u32[]{:S(2)}) copy-start(bf16[32,1,64,896]{3,2,1,0:T(8,128)(2,1)} %copy-done) | copy-start | bytes 11010052
  391.8 13.3 %copy-start.2 = (bf16[2048,2048]{1,0:T(8,128)(2,1)S(1)}, bf16[2048,2048]{1,0:T(8,128)(2,1)}, u32[]{:S(2)}) copy-start(bf16[2048,2048]{1,0:T(8,128)(2,1)} %all-gather.3.cloned.1.call-done) | copy-start | bytes 25165828
  414.5 1.8 copy-start.4
  427.3 273.3 %all-gather.5.cloned.1.call-start = ((), (), s32[]{:S(2)}) async-start(), calls=%async_computation.7 | async-start | bytes 9437184 | tf_op jit(solution)/shard_map/all_gather | solution.py:26
  700.6 12.5 %copy-start.3 = (bf16[2048,2048]{1,0:T(8,128)(2,1)S(1)}, bf16[2048,2048]{1,0:T(8,128)(2,1)}, u32[]{:S(2)}) copy-start(bf16[2048,2048]{1,0:T(8,128)(2,1)} %all-gather.5.cloned.1.call-done) | copy-start | bytes 25165828
  700.6 12.5 %copy-start.5 = (bf16[2048,896]{1,0:T(8,128)(2,1)S(1)}, bf16[2048,896]{1,0:T(8,128)(2,1)}, u32[]{:S(2)}) copy-start(bf16[2048,896]{1,0:T(8,128)(2,1)} %copy-done.4) | copy-start | bytes 11010052
Sparse Core Ops, SparseCore 0:
  118.8 146.6 reduce-scatter.2
  267.8 123.9 all-gather.2
  427.4 147.2 reduce-scatter.4
  576.7 123.9 all-gather.4
where the time goes:
time: 842 us
  waiting for transfers between devices  546 us (65%)
  blocking collectives  196 us (23%)
  matrix products  68.7 us (8%)
  between operations  14 us (2%)
  local copies, waits for them, and re-layouts  10.7 us (1%)
    reduce_scatter x2, waiting for transfers between devices, gram_matrix(): lax.psum_scatter(lax.dot_general(current, current, (((1,), (1,)), ((), ()...  294 us
    all_gather x2, waiting for transfers between devices, gram_matrix(): return lax.all_gather(owned_rows, 'mem', axis=0, tiled=True)  252 us
    all_to_all x1, blocking collectives, on_device(): lax.all_to_all(pieces.reshape(mat_count * member_count, 1, local_rows, co...  90.9 us
    all_to_all x1, blocking collectives, on_device(): lax.all_to_all(leaving.reshape(group_count * member_count, 1, local_rows,...  85.6 us
    dot_general x2, matrix products, newton_iteration(): jnp.dot(gram, current, preferred_element_type=jnp.float32)  25.8 us
    dot_general x2, matrix products, gram_matrix(): lax.dot_general(current, current, (((1,), (1,)), ((), ())), preferred_ele...  21.9 us
    dot_general x2, matrix products, newton_iteration(): second = jnp.dot(gram, product, preferred_element_type=jnp.float32)  21 us
    psum x1, blocking collectives, on_device(): sum_total = lax.psum(jnp.sum(values * values), 'mem')  19.1 us
  transfers between devices with their start and end apart: 4, of which 4 were waited for; matrix products, arithmetic and copies ran while one was open for 0% of the time, Pallas kernels for 0%

commit v1 on v0

v1 whole, which is shorter than its diff:
```python
import functools
import math

import jax
import jax.numpy as jnp
from jax import lax
from jax.experimental import pallas as pl
from jax.experimental.pallas import tpu as pltpu
from jax.sharding import Mesh, PartitionSpec as P

linear_weight = 3.4445
cubic_weight = -4.775
quintic_weight = 2.0315
epsilon = 1e-07

every = ("grp", "plane", "sub")
team = ("grp", "sub")
MIB = 1024 * 1024


def dot(a, b):
    return jnp.dot(a, b, preferred_element_type=jnp.float32)


def dot_t(a, b):
    return lax.dot_general(a, b, (((1,), (1,)), ((), ())), preferred_element_type=jnp.float32)


def params(mib):
    return pltpu.CompilerParams(vmem_limit_bytes=mib * MIB)


def device_index():
    planes = lax.axis_size("plane")
    sub = lax.axis_size("sub")
    return (lax.axis_index("grp") * planes + lax.axis_index("plane")) * sub + lax.axis_index("sub")


def member_index():
    return lax.axis_index("grp") * lax.axis_size("sub") + lax.axis_index("sub")


def in_hbm(value):
    return pltpu.with_memory_space_constraint(value, pltpu.HBM)


def in_vmem(value):
    return pltpu.with_memory_space_constraint(value, pltpu.VMEM)


HBM = pl.BlockSpec(memory_space=pltpu.HBM)
ONCHIP = pl.BlockSpec(memory_space=pltpu.VMEM)


def pack_kernel(slot_ref, x_ref, o_ref, held, load_sems, store_sems):
    outer, mats, sub, _, width = o_ref.shape
    loads = [
        pltpu.make_async_copy(x_ref.at[slot_ref[m]], held.at[m], load_sems.at[m])
        for m in range(mats)
    ]
    for load in loads[:2]:
        load.start()
    stores = []
    for m in range(mats):
        loads[m].wait()
        if m + 2 < mats:
            loads[m + 2].start()
        for g in range(outer):
            for s in range(sub):
                at = (g * sub + s) * width
                store = pltpu.make_async_copy(
                    held.at[m, :, at : at + width], o_ref.at[g, m, s], store_sems.at[len(stores)]
                )
                store.start()
                stores.append(store)
    for store in stores:
        store.wait()


def pack(iterate, slot_of, outer, sub):
    mats, rows, cols = iterate.shape
    width = cols // (outer * sub)
    return pl.pallas_call(
        pack_kernel,
        grid_spec=pltpu.PrefetchScalarGridSpec(
            num_scalar_prefetch=1,
            grid=(1,),
            in_specs=[HBM],
            out_specs=HBM,
            scratch_shapes=[
                pltpu.VMEM(iterate.shape, iterate.dtype),
                pltpu.SemaphoreType.DMA((mats,)),
                pltpu.SemaphoreType.DMA((mats * outer * sub,)),
            ],
        ),
        out_shape=pltpu.HBM((outer, mats, sub, rows, width), iterate.dtype),
        compiler_params=params(8),
        cost_estimate=pl.CostEstimate(
            flops=0, bytes_accessed=4 * iterate.size, transcendentals=0
        ),
        name="pack",
    )(in_hbm(slot_of), in_hbm(iterate))


def head_rows(width):
    return width // 2 + width // 4


def packed_rows(rows, width):
    return head_rows(width) + (rows // 2 - width) + width // 2


def write_head(o_ref, block):
    half, quarter = block.shape[0] // 2, block.shape[0] // 4
    o_ref[:half] = block[:half]
    o_ref[half : half + quarter, :half] = block[half : half + quarter, half:]
    o_ref[half : half + quarter, half:] = block[half + quarter :, half:]


def gram_strip(x_ref, d, o_ref):
    rows, _ = x_ref.shape
    blocks = lax.axis_size(team)
    width = rows // blocks
    half = blocks // 2
    head = head_rows(width)
    tail = head + (half - 1) * width
    for i in range(blocks):

        @pl.when(d == i)
        def _(i=i):
            mine = x_ref[i * width : (i + 1) * width].T
            first = min(half, blocks - i)
            value = dot(x_ref[i * width : (i + first) * width], mine).astype(o_ref.dtype)
            write_head(o_ref, value[:width])
            split = head + (first - 1) * width
            if first > 1:
                o_ref[head:split] = value[width:]
            if first < half:
                o_ref[split:tail] = dot(x_ref[: (half - first) * width], mine).astype(o_ref.dtype)
            if i < half:
                at = (i + half) * width
                last = dot(x_ref[at : at + width // 2], mine)
            else:
                at = (i - half) * width
                last = dot_t(
                    x_ref[i * width + width // 2 : (i + 1) * width], x_ref[at : at + width]
                )
            o_ref[tail:] = last.astype(o_ref.dtype)


def gram_strips(x_ref, o_ref, masks):
    index = member_index()

    @pl.loop(0, len(masks))
    def _(k):
        mask = masks[0]
        for i, value in enumerate(masks):
            mask = jnp.where(k == i, value, mask)
        gram_strip(x_ref, index ^ mask, o_ref.at[k])


def gram_kernel(masks, x_ref, o_ref):
    gram_strips(x_ref, o_ref, masks)


def gram(current, masks):
    rows, cols = current.shape
    count = len(masks)
    width = rows // lax.axis_size(team)
    packed = packed_rows(rows, width)
    return pl.pallas_call(
        functools.partial(gram_kernel, masks),
        in_specs=[ONCHIP],
        out_specs=ONCHIP,
        out_shape=pltpu.VMEM((count, packed, width), current.dtype),
        compiler_params=params(16),
        cost_estimate=pl.CostEstimate(
            flops=2 * count * packed * width * cols,
            bytes_accessed=2 * (current.size + count * packed * width),
            transcendentals=0,
        ),
        name="gram",
    )(in_vmem(current))


def add(a, b):
    return (a.astype(jnp.float32) + b.astype(jnp.float32)).astype(a.dtype)


def swap(value, mask):
    pairs = [(i, i ^ mask) for i in range(lax.axis_size(team))]
    return lax.ppermute(value, team, pairs)


def masks(sub):
    along_x, core, along_y = 1, sub, 2 * sub
    near = [0, along_x, along_y, along_x + along_y]
    return near + [core + mask for mask in near]


def scatter_sum(current, sub):
    along_x, core, along_y = 1, sub, 2 * sub
    arrived = swap(gram(current, masks(sub)[4:]), core)
    total = add(gram(current, masks(sub)[:4]), arrived)
    cut = total.shape[1] // 2
    upper, lower = total[:, :cut], total[:, cut:]
    from_x = swap(upper[1::2], along_x)
    from_y = swap(lower[2:], along_y)
    upper = add(upper[::2], from_x)
    lower = add(lower[:2], from_y)
    from_y = swap(upper[1], along_y)
    from_x = swap(lower[1], along_x)
    return add(upper[0], from_y), add(lower[0], from_x)


def gather_first(upper, lower, sub):
    along_x, core, along_y = 1, sub, 2 * sub
    lower_x = swap(lower, along_x)
    upper_y = swap(upper, along_y)
    lower_core = swap(lower, core)
    late, lower_core = lax.optimization_barrier(((upper, lower), lower_core))
    upper_x = swap(late[0], along_x)
    lower_y = swap(late[1], along_y)
    upper_xy = swap(upper_y, along_x)
    lower_xy = swap(lower_x, along_y)
    here = [upper, lower, upper_x, lower_x, upper_y, lower_y, upper_xy, lower_xy]
    return here + [swap(upper, core), lower_core] + [swap(value, core) for value in here[2:]]


def gather_second(upper, lower, strip, sub, first_work, second_work):
    along_x, core, along_y = 1, sub, 2 * sub
    dtype = strip.dtype
    lower_x = swap(lower, along_x)
    upper_y = swap(upper, along_y)
    upper_x = swap(upper, along_x)
    lower_y = swap(lower, along_y)
    other = swap(strip, core)
    result = first_work()
    lower_x, upper_y, result = lax.optimization_barrier((lower_x, upper_y, result))
    far = swap(upper_y, along_x), swap(lower_x, along_y)
    result = second_work(result)
    x = jnp.concatenate([upper_x, lower_x])
    y = jnp.concatenate([upper_y, lower_y])
    parts = [strip, other, x, y, swap(x, core), swap(y, core)]
    places = [0, core, along_x, along_y, core + along_x, core + along_y]
    far, result = lax.optimization_barrier((far, result))
    last = [swap(half, core) for half in far]
    full = spread(parts, places, dtype)
    last, full = lax.optimization_barrier((last, full))
    return full, [*far, *last], result


def block_of(index, width):
    return pl.ds(pl.multiple_of(index * width, width), width)


def fill_strip(full, strip, d, blocks, width):
    half = blocks // 2
    head = head_rows(width)
    tail = head + (half - 1) * width
    middle, quarter = width // 2, width // 4
    column = block_of(d, width)
    lower = pl.ds(pl.multiple_of(d * width + middle, middle), middle)
    full[pl.ds(pl.multiple_of(d * width, width), middle), column] = strip[:middle]
    full[lower, pl.ds(pl.multiple_of(d * width, width), middle)] = strip[:middle, middle:].T
    for i in range(2):
        at = pl.ds(pl.multiple_of(d * width + middle + i * quarter, quarter), quarter)
        full[at, lower] = strip[middle : middle + quarter, i * middle : (i + 1) * middle]
    across = strip[head:tail].T
    for k in range(1, half):
        r = block_of(lax.rem(d + k, blocks), width)
        full[r, column] = strip[head + (k - 1) * width : head + k * width]
        full[column, r] = across[:, (k - 1) * width : k * width]
    low = d < half
    c = block_of(jnp.where(low, d, d - half), width)
    start = jnp.where(low, (d + half) * width, d * width + middle)
    r = pl.ds(pl.multiple_of(start, middle), middle)
    piece = strip[tail:]
    full[r, c] = piece
    full[c, r] = piece.T


def spread_kernel(places, *refs):
    full = refs[-1]
    blocks = lax.axis_size(team)
    width = full.shape[0] // blocks
    for i, mask in enumerate(places):
        fill_strip(full, refs[i], member_index() ^ mask, blocks, width)


def spread(strips, places, dtype):
    height, width = strips[0].shape
    rows = width * lax.axis_size(team)
    return pl.pallas_call(
        functools.partial(spread_kernel, places),
        in_specs=[ONCHIP] * len(strips),
        out_specs=ONCHIP,
        out_shape=pltpu.VMEM((rows, rows), dtype),
        compiler_params=params(16),
        cost_estimate=pl.CostEstimate(
            flops=height * width * 256 * len(strips),
            bytes_accessed=6 * len(strips) * height * width,
            transcendentals=0,
        ),
        name="spread",
    )(*[in_vmem(strip) for strip in strips])


def fill_halves(full, halves, places, strip):
    blocks = lax.axis_size(team)
    width = full.shape[0] // blocks
    cut = strip.shape[0] // 2
    for i, mask in enumerate(places):
        strip[:cut] = halves[2 * i][...]
        strip[cut:] = halves[2 * i + 1][...]
        fill_strip(full, strip, member_index() ^ mask, blocks, width)


def polynomial_kernel(chunk, *refs):
    halves = refs[:-7]
    full, upper_out, lower_out, out, poly, middle, last = refs[-7:]
    rows = full.shape[0]
    packed, width = out.shape
    blocks = rows // width
    half = blocks // 2
    fill_halves(full, halves, masks(lax.axis_size("sub")), out)
    index = member_index()
    mine = block_of(index, width)

    @pl.loop(0, rows // chunk)
    def _(r):
        at = block_of(r, chunk)
        value = cubic_weight * full[at, mine].astype(jnp.float32) + quintic_weight * dot(
            full[at, :], full[:, mine]
        )
        row = lax.broadcasted_iota(jnp.int32, value.shape, 0) + r * chunk
        col = lax.broadcasted_iota(jnp.int32, value.shape, 1) + index * width
        value = value + jnp.where(row == col, linear_weight, 0.0)
        poly[at, :] = value.astype(poly.dtype)

    @pl.loop(0, rows // chunk)
    def _(r):
        at = block_of(r, chunk)
        middle[at, :] = dot(full[at, :], poly[...]).astype(middle.dtype)

    @pl.loop(0, rows // chunk)
    def _(r):
        at = block_of(r, chunk)
        poly[at, :] = (
            cubic_weight * middle[at, :].astype(jnp.float32)
            + quintic_weight * dot(full[at, :], middle[...])
        ).astype(poly.dtype)

    pair = 2 * width

    @pl.loop(0, blocks // 4 + 1)
    def _(j):
        at = block_of(lax.rem(lax.div(index, 2) + j, blocks // 2), pair)
        value = linear_weight * middle[at, :].astype(jnp.float32)
        last[at, :] = (value + dot(full[at, :], poly[...])).astype(last.dtype)

    head = head_rows(width)
    tail = head + (half - 1) * width
    write_head(out, last[mine, :])
    for k in range(1, half):
        at = block_of(lax.rem(index + k, blocks), width)
        out[head + (k - 1) * width : head + k * width] = last[at, :]
    other = pl.multiple_of(lax.rem(index + half, blocks) * width, width)

    @pl.when(index < half)
    def _():
        out[tail:] = last[pl.ds(other, width // 2), :]

    @pl.when(index >= half)
    def _():
        out[tail:] = last[pl.ds(other, width), width // 2 :].T

    upper_out[...] = out[: packed // 2]
    lower_out[...] = out[packed // 2 :]


def polynomial(halves):
    cut, width = halves[0].shape
    rows = width * len(halves) // 2
    dtype = halves[0].dtype
    return pl.pallas_call(
        functools.partial(polynomial_kernel, 1024),
        in_specs=[ONCHIP] * len(halves),
        out_specs=[ONCHIP] * 4,
        out_shape=[
            pltpu.VMEM((rows, rows), dtype),
            pltpu.VMEM((cut, width), dtype),
            pltpu.VMEM((cut, width), dtype),
            pltpu.VMEM((2 * cut, width), dtype),
        ],
        scratch_shapes=[pltpu.VMEM((rows, width), dtype)] * 3,
        compiler_params=params(16),
        cost_estimate=pl.CostEstimate(
            flops=8 * rows * rows * width, bytes_accessed=4 * rows * rows, transcendentals=0
        ),
        name="polynomial",
    )(*[in_vmem(half) for half in halves])


def columns(cols, first=0):
    return [slice(c, min(c + 256, cols)) for c in range(first, cols, 256)]


LATE = 256


def product_kernel(
    chunk, gram_ref, x_ref, o_ref, gram_out, late_out, late_product_out, late_product, sems
):
    rows, cols = o_ref.shape
    stores = [
        pltpu.make_async_copy(gram_ref, gram_out, sems.at[0]),
        pltpu.make_async_copy(x_ref.at[:, cols:], late_out, sems.at[1]),
    ]
    for store in stores:
        store.start()

    @pl.loop(0, rows // chunk)
    def _(r):
        at = block_of(r, chunk)
        late_product[at, :] = dot(gram_ref[at, :], x_ref[:, cols:]).astype(o_ref.dtype)

    stores.append(pltpu.make_async_copy(late_product, late_product_out, sems.at[2]))
    stores[2].start()

    @pl.loop(0, rows // chunk)
    def _(r):
        at = block_of(r, chunk)
        for c in columns(cols):
            o_ref[at, c] = dot(gram_ref[at, :], x_ref[:, c]).astype(o_ref.dtype)

    for store in stores:
        store.wait()


def step_start(gram_whole, current):
    rows, cols = current.shape
    dtype = current.dtype
    return pl.pallas_call(
        functools.partial(product_kernel, 1024),
        in_specs=[ONCHIP] * 2,
        out_specs=[ONCHIP, HBM, HBM, HBM],
        out_shape=[
            pltpu.VMEM((rows, cols - LATE), dtype),
            pltpu.HBM((rows, rows), dtype),
            pltpu.HBM((rows, LATE), dtype),
            pltpu.HBM((rows, LATE), dtype),
        ],
        scratch_shapes=[pltpu.VMEM((rows, LATE), dtype), pltpu.SemaphoreType.DMA((3,))],
        compiler_params=params(16),
        cost_estimate=pl.CostEstimate(
            flops=2 * rows * rows * cols, bytes_accessed=4 * rows * rows, transcendentals=0
        ),
        name="product",
    )(in_vmem(gram_whole), in_vmem(current))


def mix_kernel(chunk, gram_ref, x_ref, product_ref, o_ref):
    rows, cols = o_ref.shape

    @pl.loop(0, rows // chunk)
    def _(r):
        at = block_of(r, chunk)
        for c in columns(cols):
            second = dot(gram_ref[at, :], product_ref[:, c])
            o_ref[at, c] = mix(x_ref[at, c], product_ref[at, c], second)


def step_end(gram_whole, current, product):
    rows, cols = product.shape
    return pl.pallas_call(
        functools.partial(mix_kernel, 1024),
        in_specs=[ONCHIP] * 3,
        out_specs=ONCHIP,
        out_shape=pltpu.VMEM((rows, cols), current.dtype),
        compiler_params=params(16),
        cost_estimate=pl.CostEstimate(
            flops=2 * rows * rows * cols, bytes_accessed=2 * rows * rows, transcendentals=0
        ),
        name="mix",
    )(in_vmem(gram_whole), in_vmem(current), in_vmem(product))


SUM_ROWS = 16


def write_pieces(o_ref, value, r, chunk, local_rows, tile):
    cols = value.shape[1]
    per = chunk // local_rows
    for p in range(per):
        for t in range(cols // 128):
            o_ref[r * per + p, (tile + t) * local_rows : (tile + t + 1) * local_rows, :] = value[
                p * local_rows : (p + 1) * local_rows, t * 128 : (t + 1) * 128
            ]


def mix(current, product, second):
    return (
        linear_weight * current.astype(jnp.float32)
        + cubic_weight * product.astype(jnp.float32)
        + quintic_weight * second
    ).astype(current.dtype)


def first_part_kernel(local_rows, chunk, *refs):
    halves, x_ref = refs[:4], refs[5]
    full, gram_out, rest_out, o_ref, sum_ref, strip, product, pieces, sems = refs[6:]
    rows, cols = product.shape
    store_rest = pltpu.make_async_copy(x_ref.at[:, cols:], rest_out, sems.at[0])
    store_rest.start()
    fill_halves(full, halves, masks(lax.axis_size("sub"))[3::4], strip)
    store_gram = pltpu.make_async_copy(full, gram_out, sems.at[1])
    store_gram.start()
    sum_ref[...] = jnp.zeros_like(sum_ref)

    def stores(r):
        at = block_of(r, chunk // local_rows)
        return pltpu.make_async_copy(pieces.at[at], o_ref.at[at], sems.at[2 + r])

    @pl.loop(0, rows // chunk)
    def _(r):
        at = block_of(r, chunk)
        product[at, :] = dot(full[at, :], x_ref[:, :cols]).astype(product.dtype)

    @pl.loop(0, rows // chunk)
    def _(r):
        at = block_of(r, chunk)
        mixed = mix(x_ref[at, :cols], product[at, :], dot(full[at, :], product[...]))
        write_pieces(pieces, mixed, r, chunk, local_rows, 0)
        stores(r).start()
        value = mixed.astype(jnp.float32)
        sum_ref[...] += jnp.sum(value * value, axis=0, keepdims=True)

    store_rest.wait()
    store_gram.wait()
    for r in range(rows // chunk):
        stores(r).wait()


def first_part(full, halves, current, cols, local_rows):
    cut, width = halves[0].shape
    rows, col_count = current.shape
    dtype = current.dtype
    shape = (rows // local_rows, cols // 128 * local_rows, 128)
    return pl.pallas_call(
        functools.partial(first_part_kernel, local_rows, 1024),
        in_specs=[ONCHIP] * 6,
        out_specs=[ONCHIP, HBM, HBM, HBM, ONCHIP],
        out_shape=[
            pltpu.VMEM((rows, rows), dtype),
            pltpu.HBM((rows, rows), dtype),
            pltpu.HBM((rows, col_count - cols), dtype),
            pltpu.HBM(shape, dtype),
            pltpu.VMEM((1, cols), jnp.float32),
        ],
        input_output_aliases={4: 0},
        scratch_shapes=[
            pltpu.VMEM((2 * cut, width), dtype),
            pltpu.VMEM((rows, cols), dtype),
            pltpu.VMEM(shape, dtype),
            pltpu.SemaphoreType.DMA((2 + rows // 1024,)),
        ],
        compiler_params=params(16),
        cost_estimate=pl.CostEstimate(
            flops=4 * rows * rows * cols, bytes_accessed=4 * rows * rows, transcendentals=0
        ),
        name="first_part",
    )(*[in_vmem(half) for half in halves], in_vmem(full), in_vmem(current))[1:]


def sum_rows(total, dtype):
    high = total.astype(dtype)
    rest = jnp.where(total < jnp.inf, total - high.astype(jnp.float32), 0.0)
    middle = rest.astype(dtype)
    low = rest - middle.astype(jnp.float32)
    row = lax.broadcasted_iota(jnp.int32, (SUM_ROWS, 128), 0)
    parts = jnp.where(row == 0, high.astype(jnp.float32), 0.0)
    parts = jnp.where(row == 1, middle.astype(jnp.float32), parts)
    return jnp.where(row == 2, low, parts).astype(dtype)


def second_part_kernel(
    local_rows,
    chunk,
    before_hbm,
    late_hbm,
    late_product_hbm,
    gram_hbm,
    x_hbm,
    sum_ref,
    o_ref,
    before,
    full,
    late,
    late_product,
    x,
    product,
    total,
    pieces,
    sems,
    block_sems,
):
    rows, cols = x.shape
    count = rows // chunk
    early = cols - late.shape[1]
    body = cols // 128 * local_rows
    load_late = pltpu.make_async_copy(late_hbm, late, sems.at[0])
    load_product = pltpu.make_async_copy(late_product_hbm, late_product, sems.at[1])
    load_x = pltpu.make_async_copy(x_hbm, x.at[:, :early], sems.at[2])

    def loads(k, r):
        source, target = ((before_hbm, before), (gram_hbm, full))[k]
        at = block_of(r, chunk)
        return pltpu.make_async_copy(source.at[at, :], target.at[at, :], block_sems.at[k, r])

    def stores(r):
        at = block_of(r, chunk // local_rows)
        return pltpu.make_async_copy(
            pieces.at[at, :body, :], o_ref.at[at, :body, :], block_sems.at[2, r]
        )

    load_product.start()
    loads(0, 0).start()
    load_late.start()
    load_product.wait()
    load_late.wait()
    load_x.start()

    @pl.loop(0, count)
    def _(r):
        loads(0, r).wait()

        @pl.when(r + 1 < count)
        def _():
            loads(0, r + 1).start()

        @pl.when(r + 1 == count)
        def _():
            loads(1, 0).start()

        at = block_of(r, chunk)
        second = dot(before[at, :], late_product[...])
        x[at, early:] = mix(late[at, :], late_product[at, :], second)

    load_x.wait()

    @pl.loop(0, count)
    def _(r):
        loads(1, r).wait()

        @pl.when(r + 1 < count)
        def _():
            loads(1, r + 1).start()

        at = block_of(r, chunk)
        for c in columns(cols):
            product[at, c] = dot(full[at, :], x[:, c]).astype(product.dtype)

    total[...] = jnp.zeros_like(total)

    @pl.loop(0, count)
    def _(r):
        at = block_of(r, chunk)
        for c in columns(cols):
            mixed = mix(x[at, c], product[at, c], dot(full[at, :], product[:, c]))
            write_pieces(pieces, mixed, r, chunk, local_rows, c.start // 128)
            value = mixed.astype(jnp.float32)
            total[:, c] += jnp.sum(value * value, axis=0, keepdims=True)
        stores(r).start()

    tail = sum_rows(
        jnp.sum(total[...], axis=1, keepdims=True)
        + jnp.sum(sum_ref[...], axis=1, keepdims=True),
        o_ref.dtype,
    )
    for p in range(o_ref.shape[0]):
        pieces[p, body:, :] = tail
    store = pltpu.make_async_copy(pieces.at[:, body:, :], o_ref.at[:, body:, :], sems.at[3])
    store.start()
    for r in range(count):
        stores(r).wait()
    store.wait()


def second_part(before, late, late_product, gram_whole, current, sums, local_rows):
    rows, early = current.shape
    cols = early + late.shape[1]
    dtype = current.dtype
    chunk = 512
    shape = (rows // local_rows, cols // 128 * local_rows + SUM_ROWS, 128)
    return pl.pallas_call(
        functools.partial(second_part_kernel, local_rows, chunk),
        in_specs=[HBM] * 5 + [ONCHIP],
        out_specs=HBM,
        out_shape=pltpu.HBM(shape, dtype),
        scratch_shapes=[
            pltpu.VMEM((rows, rows), dtype),
            pltpu.VMEM((rows, rows), dtype),
            pltpu.VMEM(late.shape, dtype),
            pltpu.VMEM(late.shape, dtype),
            pltpu.VMEM((rows, cols), dtype),
            pltpu.VMEM((rows, cols), dtype),
            pltpu.VMEM((1, cols), jnp.float32),
            pltpu.VMEM(shape, dtype),
            pltpu.SemaphoreType.DMA((4,)),
            pltpu.SemaphoreType.DMA((3, rows // chunk)),
        ],
        compiler_params=params(40),
        cost_estimate=pl.CostEstimate(
            flops=4 * rows * rows * (cols + late.shape[1]),
            bytes_accessed=8 * rows * rows,
            transcendentals=0,
        ),
        name="second_part",
    )(
        *[in_hbm(value) for value in (before, late, late_product, gram_whole, current)],
        in_vmem(sums),
    )


def scaled_kernel(target, first_ref, second_ref, o_ref):
    outer, _, sub, _, _ = first_ref.shape
    local_rows = o_ref.shape[1]
    tiles = first_ref.shape[3] // local_rows
    more = second_ref.shape[3] // local_rows
    total = jnp.zeros((1, 128), jnp.float32)
    for g in range(outer):
        for s in range(sub):
            parts = second_ref[g, 0, s, more * local_rows :, :].astype(jnp.float32)
            total = total + jnp.sum(parts, axis=0, keepdims=True)
    scale = target / (jnp.sqrt(total) + epsilon)
    at = 0
    for g in range(outer):
        for s in range(sub):
            for t in range(tiles + more):
                if t < tiles:
                    value = first_ref[g, 0, s, t * local_rows : (t + 1) * local_rows, :]
                else:
                    u = t - tiles
                    value = second_ref[g, 0, s, u * local_rows : (u + 1) * local_rows, :]
                o_ref[0, :, at : at + 128] = (value.astype(jnp.float32) * scale).astype(
                    o_ref.dtype
                )
                at += 128


def scaled(first, second, local_rows, target):
    outer, mats, sub, height, _ = first.shape
    height_more = second.shape[3]
    cols = outer * sub * 128 * (height // local_rows + height_more // local_rows)
    return pl.pallas_call(
        functools.partial(scaled_kernel, target),
        grid=(mats,),
        in_specs=[
            pl.BlockSpec((outer, 1, sub, height, 128), lambda m: (0, m, 0, 0, 0)),
            pl.BlockSpec((outer, 1, sub, height_more, 128), lambda m: (0, m, 0, 0, 0)),
        ],
        out_specs=pl.BlockSpec((1, local_rows, cols), lambda m: (m, 0, 0)),
        out_shape=jax.ShapeDtypeStruct((mats, local_rows, cols), first.dtype),
        compiler_params=params(14),
        cost_estimate=pl.CostEstimate(
            flops=first.size + second.size,
            bytes_accessed=4 * (first.size + second.size),
            transcendentals=0,
        ),
        name="scaled",
    )(first, second)


def plain_strip(gram, index, width):
    strip = lax.dynamic_slice_in_dim(gram, index * width, width, axis=1)
    row = lax.broadcasted_iota(jnp.int32, strip.shape, 0)
    col = lax.broadcasted_iota(jnp.int32, strip.shape, 1) + index * width
    poly = (
        jnp.where(row == col, linear_weight, 0.0)
        + cubic_weight * strip.astype(jnp.float32)
        + quintic_weight * dot(gram, strip)
    ).astype(jnp.bfloat16)
    middle = dot(gram, poly).astype(jnp.bfloat16)
    middle_f = middle.astype(jnp.float32)
    inner = (cubic_weight * middle_f + quintic_weight * dot(gram, middle)).astype(jnp.bfloat16)
    return (linear_weight * middle_f + dot(gram, inner)).astype(jnp.bfloat16)


def plain_step(gram, current):
    product = dot(gram, current).astype(jnp.bfloat16)
    return mix(current, product, dot(gram, product))


def exchange(pieces):
    return lax.all_to_all(pieces, every, split_axis=0, concat_axis=0, tiled=True)


def kernel_path(iterate, slot_of, outer, groups, sub):
    members = outer * sub
    mats, local_rows, col_count = iterate.shape
    col_width = col_count // members
    rows = local_rows * groups * members
    pieces = pack(iterate, slot_of, outer, sub)
    arrived = exchange(pieces.reshape(mats * members, local_rows, col_width))
    current = arrived.reshape(rows, col_width)
    gram_whole, upper, lower, strip = polynomial(gather_first(*scatter_sum(current, sub), sub))

    def first_work():
        return step_start(gram_whole, current)

    def second_work(done):
        product, *kept = done
        return step_end(gram_whole, current, product), kept

    full, halves, (stepped, kept) = gather_second(
        upper, lower, strip, sub, first_work, second_work
    )
    whole, rest, first, sums = first_part(full, halves, stepped, 256, local_rows)
    first = exchange(first)
    second = exchange(second_part(*kept, whole, rest, sums, local_rows))
    return scaled(
        first.reshape(outer, mats, sub, -1, 128),
        second.reshape(outer, mats, sub, -1, 128),
        local_rows,
        math.sqrt(rows * col_count),
    )


def plain_path(iterate, slot_of, outer, groups, sub):
    members = outer * sub
    mats, local_rows, col_count = iterate.shape
    col_width = col_count // members
    rows = local_rows * groups * members
    pieces = jnp.take(iterate, slot_of, axis=0)
    pieces = pieces.reshape(mats, local_rows, outer, sub, col_width).transpose(2, 0, 3, 1, 4)
    arrived = exchange(pieces.reshape(mats * members, local_rows, col_width))
    current = arrived.reshape(rows, col_width)
    partial = dot_t(current, current).astype(jnp.bfloat16)
    owned = lax.psum_scatter(partial, team, scatter_dimension=0, tiled=True)
    gram = lax.all_gather(owned, team, axis=0, tiled=True)
    strip = plain_strip(gram, lax.axis_index(team), rows // members)
    gram_next = lax.all_gather(strip.T, team, axis=0, tiled=True)
    current = plain_step(gram, current)
    current = plain_step(gram_next, current)
    values = current.astype(jnp.float32)
    sum_total = lax.psum(jnp.sum(values * values), team)
    scale = math.sqrt(rows * col_count) / (jnp.sqrt(sum_total) + epsilon)
    leaving = (values * scale).astype(jnp.bfloat16)
    returned = exchange(leaving.reshape(groups * members, local_rows, col_width))
    returned = returned.reshape(outer, mats, sub, local_rows, col_width)
    return returned.transpose(1, 3, 0, 2, 4).reshape(mats, local_rows, col_count)


def on_device(iterate, slot_of):
    groups = lax.axis_size("plane")
    sub = lax.axis_size("sub")
    outer = lax.axis_size("grp")
    members = outer * sub
    _, local_rows, col_count = iterate.shape
    col_width = col_count // members
    strip_width = local_rows * groups
    fits = (
        col_width % 128 == 0
        and col_width > 256 + LATE
        and strip_width % 256 == 0
        and local_rows % 16 == 0
        and sub == 2
        and outer == 4
        and groups == 4
    )
    return (kernel_path if fits else plain_path)(iterate, slot_of, outer, groups, sub)


def solution(mesh):
    outer, inner = mesh.devices.shape
    split = Mesh(mesh.devices.reshape(outer, outer, inner // outer), every)
    spec = P(None, every, None)
    return jax.shard_map(
        on_device,
        mesh=split,
        in_specs=(spec, P()),
        out_specs=spec,
        check_vma=False,
    )
```

time: 842 us -> 298 us (0.35)
  waiting for transfers between devices: 546 us -> 41.6 us
  Pallas kernels: 0 us -> 75.8 us
  matrix products: 68.7 us -> 0 us
  blocking collectives: 196 us -> 158 us
  starting transfers between devices: 0.3 us -> 20 us
  between operations: 14 us -> 0.26 us
  local copies, waits for them, and re-layouts: 10.7 us -> 0.27 us
    reduce_scatter x2 -> x0, waiting for transfers between devices: 294 us -> none  [gram_matrix(): lax.psum_scatter(lax.dot_general(current, current, (((1,), (1,)), ((), ()...]
    all_gather x2 -> x0, waiting for transfers between devices: 252 us -> none  [gram_matrix(): return lax.all_gather(owned_rows, 'mem', axis=0, tiled=True)]
    pallas_call x0 -> x10, Pallas kernels: none -> 75.8 us  [the longest x1 24.8 us: second_part(): pl.pallas_call(functools.partial(second_part_kernel, local_rows, chunk),...]
    dot_general x6 -> x0, matrix products: 68.7 us -> none  [the longest x2 25.8 us: newton_iteration(): jnp.dot(gram, current, preferred_element_type=jnp.float32)]
    ppermute x0 -> x30, waiting for transfers between devices: none -> 39.1 us  [swap(): return lax.ppermute(value, team, pairs)]
    psum x1 -> x0, blocking collectives: 19.1 us -> none  [on_device(): sum_total = lax.psum(jnp.sum(values * values), 'mem')]
    all_to_all x2, blocking collectives: 176 us -> 158 us  [exchange(): lax.all_to_all(pieces, every, split_axis=0, concat_axis=0, tiled=True)]
    ppermute x0 -> x30, starting transfers between devices: none -> 17 us  [swap(): return lax.ppermute(value, team, pairs)]
  transfers between devices with their start and end apart: 4 -> 31, of which waited for: 4 -> 15; matrix products, arithmetic and copies ran while one was open for 0% -> 0% of each run, Pallas kernels for 0% -> 15%
where the time goes in v1:
time: 298 us; the launch traced here: 297 us
  blocking collectives  158 us (53%)
  Pallas kernels  75.8 us (25%)
  waiting for transfers between devices  41.6 us (14%)
  starting transfers between devices  20 us (7%)
    all_to_all x2, blocking collectives, exchange(): lax.all_to_all(pieces, every, split_axis=0, concat_axis=0, tiled=True)  158 us
    ppermute x30, waiting for transfers between devices, swap(): return lax.ppermute(value, team, pairs)  39.1 us
    pallas_call x1, Pallas kernels, second_part(): pl.pallas_call(functools.partial(second_part_kernel, local_rows, chunk),...  24.8 us
    ppermute x30, starting transfers between devices, swap(): return lax.ppermute(value, team, pairs)  17 us
    pallas_call x1, Pallas kernels, polynomial(): pl.pallas_call(functools.partial(polynomial_kernel, 1024), in_specs=[ONCH...  11.6 us
    pallas_call x1, Pallas kernels, step_start(): pl.pallas_call(functools.partial(product_kernel, 1024), in_specs=[ONCHIP]...  9.36 us
    pallas_call x2, Pallas kernels, gram(): pl.pallas_call(functools.partial(gram_kernel, masks), in_specs=[ONCHIP],...  7.32 us
    pallas_call x1, Pallas kernels, step_end(): pl.pallas_call(functools.partial(mix_kernel, 1024), in_specs=[ONCHIP] * 3...  6.97 us
  transfers between devices with their start and end apart: 31, of which 15 were waited for; matrix products, arithmetic and copies ran while one was open for 0% of the time, Pallas kernels for 15%

profile of v1, /device:TPU:0, one launch (start us, length us, event | category | flops | bytes accessed | tf_op | source)
XLA Modules:
  0.0 297.2 jit_solution(8673867082491662002)
XLA Ops:
  0.0 5.3 %pack.1 = bf16[4,4,2,64,896]{4,3,2,1,0:T(8,128)(2,1)} custom-call(s32[4]{0:T(128)} %slot_ref.1, bf16[4,64,7168]{2,1,0:T(8,128)(2,1)} %x_ref.1), custom_call_target="tpu_custom_call" | custom-call | bytes 7340032 | tf_op jit(solution)/shard_map/pack/pallas_call | solution.py:83
  5.3 91.1 %all_to_all.15 = bf16[32,64,896]{2,1,0:T(8,128)(2,1)S(1)} all-to-all(bf16[32,64,896]{2,1,0:T(8,128)(2,1)} %bitcast.24), channel_id=1, replica_groups=mesh['grp'=4,'plane'=4,'sub'=2] {'grp','plane','sub'}, dimensions={0} | all-to-all | bytes 7340032 | tf_op jit(solution)/shard_map/all_to_all | solution.py:796
  96.3 3.6 %gram.3 = bf16[4,1088,256]{2,1,0:T(8,128)(2,1)S(1)} custom-call(bf16[2048,896]{1,0:T(8,128)(2,1)S(1)} %bitcast.20), custom_call_target="tpu_custom_call" | custom-call | flops 1996488704 | bytes 5898240 | tf_op jit(solution)/shard_map/gram/pallas_call | solution.py:171
  100.0 3.8 %gram.2 = bf16[4,1088,256]{2,1,0:T(8,128)(2,1)S(1)} custom-call(bf16[2048,896]{1,0:T(8,128)(2,1)S(1)} %bitcast.21), custom_call_target="tpu_custom_call" | custom-call | flops 1996488704 | bytes 5898240 | tf_op jit(solution)/shard_map/gram/pallas_call | solution.py:171
  105.6 0.9 collective-permute-start.1
  106.5 13.1 %collective-permute-done.3 = bf16[2,544,256]{2,1,0:T(8,128)(2,1)S(1)} collective-permute-done((bf16[2,544,256]{2,1,0:T(8,128)(2,1)S(1)}, bf16[2,544,256]{2,1,0:T(8,128)(2,1)S(1)}, u32[]{:S(2)}, u32[]{:S(2)}) %collective-permute-start.3) | collective-permute-done | bytes 557088 | tf_op jit(solution)/shard_map/ppermute | solution.py:192
  119.8 0.9 collective-permute-start.4
  120.9 0.9 collective-permute-start.2
  121.8 5.9 %collective-permute-done.4 = bf16[544,256]{1,0:T(8,128)(2,1)S(1)} collective-permute-done((bf16[544,256]{1,0:T(8,128)(2,1)S(1)}, bf16[544,256]{1,0:T(8,128)(2,1)S(1)}, u32[]{:S(2)}, u32[]{:S(2)}) %collective-permute-start.4) | collective-permute-done | bytes 278560 | tf_op jit(solution)/shard_map/ppermute | solution.py:192
  127.8 0.9 collective-permute-start.7
  130.3 4.5 %collective-permute-done.7.refs_3_ = bf16[544,256]{1,0:T(8,128)(2,1)S(1)} collective-permute-done((bf16[544,256]{1,0:T(8,128)(2,1)S(1)}, bf16[544,256]{1,0:T(8,128)(2,1)S(1)}, u32[]{:S(2)}, u32[]{:S(2)}) %collective-permute-start.7) | collective-permute-done | bytes 278560 | tf_op jit(solution)/shard_map/ppermute | solution.py:192
  134.8 1.1 collective-permute-start.11
  136.2 1.5 collective-permute-start.9
  138.0 1.5 collective-permute-start.10
  139.6 4.7 %collective-permute-done.11.refs_7_ = bf16[544,256]{1,0:T(8,128)(2,1)S(1)} collective-permute-done((bf16[544,256]{1,0:T(8,128)(2,1)S(1)}, bf16[544,256]{1,0:T(8,128)(2,1)S(1)}, u32[]{:S(2)}, u32[]{:S(2)}) %collective-permute-start.11) | collective-permute-done | bytes 278560 | tf_op jit(solution)/shard_map/ppermute | solution.py:192
  144.3 1.1 collective-permute-done.6.refs_2_
  145.4 4.5 %collective-permute-done.9.refs_5_ = bf16[544,256]{1,0:T(8,128)(2,1)S(1)} collective-permute-done((bf16[544,256]{1,0:T(8,128)(2,1)S(1)}, bf16[544,256]{1,0:T(8,128)(2,1)S(1)}, u32[]{:S(2)}, u32[]{:S(2)}) %collective-permute-start.9) | collective-permute-done | bytes 278560 | tf_op jit(solution)/shard_map/ppermute | solution.py:192
  152.2 11.6 %polynomial.1 = (bf16[2048,2048]{1,0:T(8,128)(2,1)S(1)}, bf16[544,256]{1,0:T(8,128)(2,1)S(1)}, bf16[544,256]{1,0:T(8,128)(2,1)S(1)}, bf16[1088,256]{1,0:T(8,128)(2,1)S(1)}) custom-call(bf16[544,256]{1,0:T(8,128)(2,1)S(1)} %fusion.1.refs_0_, bf16[544,256]{1,0:T(8,128)(2,1)S(1)} %fusion.refs_1_, bf16[544,256]{1,0:T(8,128)(2,1)S(1)} %collective-permute-done.6.refs_2_, ...), custom_call_target="tpu_custom_call" | custom-call | flops 8589934592 | bytes 16777216 | tf_op jit(solution)/shard_map/polynomial/pallas_call | solution.py:386
  163.8 1.1 collective-permute-start.27
  165.8 1.2 collective-permute-start.26
  166.9 1.0 collective-permute-start.20
  168.0 9.4 %product.1 = (bf16[2048,640]{1,0:T(8,128)(2,1)S(1)}, bf16[2048,2048]{1,0:T(8,128)(2,1)}, bf16[2048,256]{1,0:T(8,128)(2,1)}, bf16[2048,256]{1,0:T(8,128)(2,1)}) custom-call(bf16[2048,2048]{1,0:T(8,128)(2,1)S(1)} %get-tuple-element.40.gram_ref, bf16[2048,896]{1,0:T(8,128)(2,1)S(1)} %bitcast.22), custom_call_target="tpu_custom_call" | custom-call | flops 7516192768 | bytes 16777216 | tf_op jit(solution)/shard_map/product/pallas_call | solution.py:444
  177.3 1.3 collective-permute-done.20
  179.5 1.1 collective-permute-start.22
  181.2 7.0 %mix.1.refs_5_ = bf16[2048,640]{1,0:T(8,128)(2,1)S(1)} custom-call(bf16[2048,2048]{1,0:T(8,128)(2,1)S(1)} %get-tuple-element.40.gram_ref, bf16[2048,896]{1,0:T(8,128)(2,1)S(1)} %bitcast.23, bf16[2048,640]{1,0:T(8,128)(2,1)S(1)} %get-tuple-element.47.product_ref), custom_call_target="tpu_custom_call" | custom-call | flops 5368709120 | bytes 8388608 | tf_op jit(solution)/shard_map/mix/pallas_call | solution.py:476
  188.8 1.2 spread.1.refs_4_
  190.2 6.6 %first_part.1 = (bf16[2048,2048]{1,0:T(8,128)(2,1)S(1)}, bf16[2048,2048]{1,0:T(8,128)(2,1)}, bf16[2048,384]{1,0:T(8,128)(2,1)}, bf16[32,128,128]{2,1,0:T(8,128)(2,1)}, f32[1,256]{1,0:T(1,128)S(1)}) custom-call(bf16[544,256]{1,0:T(8,128)(2,1)S(1)} %collective-permute-done.21.refs_0_, ...), custom_call_target="tpu_custom_call", output_to_operand_aliasing={{0}: (4, {})} | custom-call | flops 4294967296 | bytes 16777216 | tf_op jit(solution)/shard_map/first_part/pallas_call | solution.py:550
  196.8 3.1 %all-to-all-start.1 = ((bf16[32,128,128]{2,1,0:T(8,128)(2,1)}), bf16[32,128,128]{2,1,0:T(8,128)(2,1)S(1)}, u32[]{:S(2)}, u32[]{:S(2)}) async-start(bf16[32,128,128]{2,1,0:T(8,128)(2,1)} %get-tuple-element.58), calls=%async_computation.1 | async-start | bytes 2097152 | tf_op jit(solution)/shard_map/all_to_all | solution.py:796
  199.9 24.8 %second_part.1 = bf16[32,336,128]{2,1,0:T(8,128)(2,1)} custom-call(bf16[2048,2048]{1,0:T(8,128)(2,1)} %get-tuple-element.59.before_hbm, bf16[2048,256]{1,0:T(8,128)(2,1)} %get-tuple-element.60.late_hbm, bf16[2048,256]{1,0:T(8,128)(2,1)} %get-tuple-element.61.late_product_hbm, bf16[2048,2048]{1,0:T(8,128)(2,1)} %get-tuple-element.62.gram_hbm, ...), custom_call_target="tpu_custom_call" | custom-call | flops 15032385536 | bytes 33554432 | tf_op jit(solution)/shard_map/second_part/pallas_call | solution.py:696
  224.7 2.5 all-to-all-done.1
  227.2 67.2 %all_to_all.16 = bf16[32,336,128]{2,1,0:T(8,128)(2,1)S(1)} all-to-all(bf16[32,336,128]{2,1,0:T(8,128)(2,1)} %second_part.1), channel_id=1, replica_groups=mesh['grp'=4,'plane'=4,'sub'=2] {'grp','plane','sub'}, dimensions={0} | all-to-all | bytes 5505024 | tf_op jit(solution)/shard_map/all_to_all | solution.py:796
  294.4 2.8 scaled.1
  (56 shorter events, 10.0 us)
Async XLA Ops:
  99.9 4.4 %collective-permute-start = (bf16[4,1088,256]{2,1,0:T(8,128)(2,1)S(1)}, bf16[4,1088,256]{2,1,0:T(8,128)(2,1)S(1)}, u32[]{:S(2)}, u32[]{:S(2)}) collective-permute-start(bf16[4,1088,256]{2,1,0:T(8,128)(2,1)S(1)} %gram.3), channel_id=1, source_target_pairs={{0,8},{1,9},{8,0},{9,1},{16,24},{17,25},{24,16},{25,17},{2,10},{3,... | collective-permute-start | bytes 6684680 | tf_op jit(solution)/shard_map/ppermute | solution.py:192
  104.9 14.7 %collective-permute-start.3 = (bf16[2,544,256]{2,1,0:T(8,128)(2,1)S(1)}, bf16[2,544,256]{2,1,0:T(8,128)(2,1)S(1)}, u32[]{:S(2)}, u32[]{:S(2)}) collective-permute-start(bf16[2,544,256]{2,1,0:T(8,128)(2,1)S(1)} %slice.43), channel_id=1, source_target_pairs={{0,16},{1,17},{8,24},{9,25},{16,0},{17,1},{24,8},{25,9},{2,18},{3,... | collective-permute-start | bytes 1671176 | tf_op jit(solution)/shard_map/ppermute | solution.py:192
  105.6 15.1 %collective-permute-start.1 = (bf16[2,544,256]{2,1,0:T(8,128)(2,1)S(1)}, bf16[2,544,256]{2,1,0:T(8,128)(2,1)S(1)}, u32[]{:S(2)}, u32[]{:S(2)}) collective-permute-start(bf16[2,544,256]{2,1,0:T(8,128)(2,1)S(1)} %slice.32), channel_id=1, source_target_pairs={{0,1},{1,0},{8,9},{9,8},{16,17},{17,16},{24,25},{25,24},{2,3},{3,2... | collective-permute-start | bytes 1671176 | tf_op jit(solution)/shard_map/ppermute | solution.py:192
  119.8 7.9 %collective-permute-start.4 = (bf16[544,256]{1,0:T(8,128)(2,1)S(1)}, bf16[544,256]{1,0:T(8,128)(2,1)S(1)}, u32[]{:S(2)}, u32[]{:S(2)}) collective-permute-start(bf16[544,256]{1,0:T(8,128)(2,1)S(1)} %slice_bitcast_fusion), channel_id=1, source_target_pairs={{0,1},{1,0},{8,9},{9,8},{16,17},{17,16},{24,25},{25,24},{2,3},{3,2... | collective-permute-start | bytes 835592 | tf_op jit(solution)/shard_map/ppermute | solution.py:192
  120.9 7.8 %collective-permute-start.2 = (bf16[544,256]{1,0:T(8,128)(2,1)S(1)}, bf16[544,256]{1,0:T(8,128)(2,1)S(1)}, u32[]{:S(2)}, u32[]{:S(2)}) collective-permute-start(bf16[544,256]{1,0:T(8,128)(2,1)S(1)} %slice_bitcast_fusion.2), channel_id=1, source_target_pairs={{0,16},{1,17},{8,24},{9,25},{16,0},{17,1},{24,8},{25,9},{2,18},{3,... | collective-permute-start | bytes 835592 | tf_op jit(solution)/shard_map/ppermute | solution.py:192
  127.8 7.0 %collective-permute-start.7 = (bf16[544,256]{1,0:T(8,128)(2,1)S(1)}, bf16[544,256]{1,0:T(8,128)(2,1)S(1)}, u32[]{:S(2)}, u32[]{:S(2)}) collective-permute-start(bf16[544,256]{1,0:T(8,128)(2,1)S(1)} %fusion.refs_1_), channel_id=1, source_target_pairs={{0,1},{1,0},{8,9},{9,8},{16,17},{17,16},{24,25},{25,24},{2,3},{3,2... | collective-permute-start | bytes 835592 | tf_op jit(solution)/shard_map/ppermute | solution.py:192
  128.7 1.6 collective-permute-start.5
  128.8 7.4 %collective-permute-start.12 = (bf16[544,256]{1,0:T(8,128)(2,1)S(1)}, bf16[544,256]{1,0:T(8,128)(2,1)S(1)}, u32[]{:S(2)}, u32[]{:S(2)}) collective-permute-start(bf16[544,256]{1,0:T(8,128)(2,1)S(1)} %fusion.1.refs_0_), channel_id=1, source_target_pairs={{0,8},{1,9},{8,0},{9,1},{16,24},{17,25},{24,16},{25,17},{2,10},{3,... | collective-permute-start | bytes 835592 | tf_op jit(solution)/shard_map/ppermute | solution.py:192
  129.4 8.7 %collective-permute-start.8 = (bf16[544,256]{1,0:T(8,128)(2,1)S(1)}, bf16[544,256]{1,0:T(8,128)(2,1)S(1)}, u32[]{:S(2)}, u32[]{:S(2)}) collective-permute-start(bf16[544,256]{1,0:T(8,128)(2,1)S(1)} %fusion.1.refs_0_), channel_id=1, source_target_pairs={{0,16},{1,17},{8,24},{9,25},{16,0},{17,1},{24,8},{25,9},{2,18},{3,... | collective-permute-start | bytes 835592 | tf_op jit(solution)/shard_map/ppermute | solution.py:192
  134.8 4.7 %collective-permute-start.14 = (bf16[544,256]{1,0:T(8,128)(2,1)S(1)}, bf16[544,256]{1,0:T(8,128)(2,1)S(1)}, u32[]{:S(2)}, u32[]{:S(2)}) collective-permute-start(bf16[544,256]{1,0:T(8,128)(2,1)S(1)} %collective-permute-done.7.refs_3_), channel_id=1, source_target_pairs={{0,8},{1,9},{8,0},{9,1},{16,24},{17,25},{24,16},{25,17},{2,10},{3,... | collective-permute-start | bytes 835592 | tf_op jit(solution)/shard_map/ppermute | solution.py:192
  134.8 9.5 %collective-permute-start.11 = (bf16[544,256]{1,0:T(8,128)(2,1)S(1)}, bf16[544,256]{1,0:T(8,128)(2,1)S(1)}, u32[]{:S(2)}, u32[]{:S(2)}) collective-permute-start(bf16[544,256]{1,0:T(8,128)(2,1)S(1)} %collective-permute-done.7.refs_3_), channel_id=1, source_target_pairs={{0,16},{1,17},{8,24},{9,25},{16,0},{17,1},{24,8},{25,9},{2,18},{3,... | collective-permute-start | bytes 835592 | tf_op jit(solution)/shard_map/ppermute | solution.py:192
  135.9 9.5 %collective-permute-start.6 = (bf16[544,256]{1,0:T(8,128)(2,1)S(1)}, bf16[544,256]{1,0:T(8,128)(2,1)S(1)}, u32[]{:S(2)}, u32[]{:S(2)}) collective-permute-start(bf16[544,256]{1,0:T(8,128)(2,1)S(1)} %fusion.1.refs_0_), channel_id=1, source_target_pairs={{0,1},{1,0},{8,9},{9,8},{16,17},{17,16},{24,25},{25,24},{2,3},{3,2... | collective-permute-start | bytes 835592 | tf_op jit(solution)/shard_map/ppermute | solution.py:192
  136.2 13.8 %collective-permute-start.9 = (bf16[544,256]{1,0:T(8,128)(2,1)S(1)}, bf16[544,256]{1,0:T(8,128)(2,1)S(1)}, u32[]{:S(2)}, u32[]{:S(2)}) collective-permute-start(bf16[544,256]{1,0:T(8,128)(2,1)S(1)} %fusion.refs_1_), channel_id=1, source_target_pairs={{0,16},{1,17},{8,24},{9,25},{16,0},{17,1},{24,8},{25,9},{2,18},{3,... | collective-permute-start | bytes 835592 | tf_op jit(solution)/shard_map/ppermute | solution.py:192
  138.0 12.6 %collective-permute-start.10 = (bf16[544,256]{1,0:T(8,128)(2,1)S(1)}, bf16[544,256]{1,0:T(8,128)(2,1)S(1)}, u32[]{:S(2)}, u32[]{:S(2)}) collective-permute-start(bf16[544,256]{1,0:T(8,128)(2,1)S(1)} %collective-permute-done.8.refs_4_), channel_id=1, source_target_pairs={{0,1},{1,0},{8,9},{9,8},{16,17},{17,16},{24,25},{25,24},{2,3},{3,2... | collective-permute-start | bytes 835592 | tf_op jit(solution)/shard_map/ppermute | solution.py:192
  139.6 11.1 %collective-permute-start.15 = (bf16[544,256]{1,0:T(8,128)(2,1)S(1)}, bf16[544,256]{1,0:T(8,128)(2,1)S(1)}, u32[]{:S(2)}, u32[]{:S(2)}) collective-permute-start(bf16[544,256]{1,0:T(8,128)(2,1)S(1)} %collective-permute-done.8.refs_4_), channel_id=1, source_target_pairs={{0,8},{1,9},{8,0},{9,1},{16,24},{17,25},{24,16},{25,17},{2,10},{3,... | collective-permute-start | bytes 835592 | tf_op jit(solution)/shard_map/ppermute | solution.py:192
  144.3 6.4 %collective-permute-start.18 = (bf16[544,256]{1,0:T(8,128)(2,1)S(1)}, bf16[544,256]{1,0:T(8,128)(2,1)S(1)}, u32[]{:S(2)}, u32[]{:S(2)}) collective-permute-start(bf16[544,256]{1,0:T(8,128)(2,1)S(1)} %collective-permute-done.11.refs_7_), channel_id=1, source_target_pairs={{0,8},{1,9},{8,0},{9,1},{16,24},{17,25},{24,16},{25,17},{2,10},{3,... | collective-permute-start | bytes 835592 | tf_op jit(solution)/shard_map/ppermute | solution.py:192
  145.4 5.3 %collective-permute-start.13 = (bf16[544,256]{1,0:T(8,128)(2,1)S(1)}, bf16[544,256]{1,0:T(8,128)(2,1)S(1)}, u32[]{:S(2)}, u32[]{:S(2)}) collective-permute-start(bf16[544,256]{1,0:T(8,128)(2,1)S(1)} %collective-permute-done.6.refs_2_), channel_id=1, source_target_pairs={{0,8},{1,9},{8,0},{9,1},{16,24},{17,25},{24,16},{25,17},{2,10},{3,... | collective-permute-start | bytes 835592 | tf_op jit(solution)/shard_map/ppermute | solution.py:192
  150.0 1.6 collective-permute-start.16
  150.7 1.6 collective-permute-start.17
  163.8 16.8 %collective-permute-start.27 = (bf16[544,256]{1,0:T(8,128)(2,1)S(1)}, bf16[544,256]{1,0:T(8,128)(2,1)S(1)}, u32[]{:S(2)}, u32[]{:S(2)}) collective-permute-start(bf16[544,256]{1,0:T(8,128)(2,1)S(1)} %get-tuple-element.38), channel_id=1, source_target_pairs={{0,16},{1,17},{8,24},{9,25},{16,0},{17,1},{24,8},{25,9},{2,18},{3,... | collective-permute-start | bytes 835592 | tf_op jit(solution)/shard_map/ppermute | solution.py:192
  164.9 12.4 %collective-permute-start.19 = (bf16[544,256]{1,0:T(8,128)(2,1)S(1)}, bf16[544,256]{1,0:T(8,128)(2,1)S(1)}, u32[]{:S(2)}, u32[]{:S(2)}) collective-permute-start(bf16[544,256]{1,0:T(8,128)(2,1)S(1)} %get-tuple-element.38), channel_id=1, source_target_pairs={{0,1},{1,0},{8,9},{9,8},{16,17},{17,16},{24,25},{25,24},{2,3},{3,2... | collective-permute-start | bytes 835592 | tf_op jit(solution)/shard_map/ppermute | solution.py:192
  165.8 14.8 %collective-permute-start.26 = (bf16[544,256]{1,0:T(8,128)(2,1)S(1)}, bf16[544,256]{1,0:T(8,128)(2,1)S(1)}, u32[]{:S(2)}, u32[]{:S(2)}) collective-permute-start(bf16[544,256]{1,0:T(8,128)(2,1)S(1)} %get-tuple-element.39), channel_id=1, source_target_pairs={{0,1},{1,0},{8,9},{9,8},{16,17},{17,16},{24,25},{25,24},{2,3},{3,2... | collective-permute-start | bytes 835592 | tf_op jit(solution)/shard_map/ppermute | solution.py:192
  166.9 11.6 %collective-permute-start.20 = (bf16[544,256]{1,0:T(8,128)(2,1)S(1)}, bf16[544,256]{1,0:T(8,128)(2,1)S(1)}, u32[]{:S(2)}, u32[]{:S(2)}) collective-permute-start(bf16[544,256]{1,0:T(8,128)(2,1)S(1)} %get-tuple-element.39), channel_id=1, source_target_pairs={{0,16},{1,17},{8,24},{9,25},{16,0},{17,1},{24,8},{25,9},{2,18},{3,... | collective-permute-start | bytes 835592 | tf_op jit(solution)/shard_map/ppermute | solution.py:192
  167.9 20.9 %collective-permute-start.25 = (bf16[1088,256]{1,0:T(8,128)(2,1)S(1)}, bf16[1088,256]{1,0:T(8,128)(2,1)S(1)}, u32[]{:S(2)}, u32[]{:S(2)}) collective-permute-start(bf16[1088,256]{1,0:T(8,128)(2,1)S(1)} %get-tuple-element.53.refs_0_), channel_id=1, source_target_pairs={{0,8},{1,9},{8,0},{9,1},{16,24},{17,25},{24,16},{25,17},{2,10},{3,... | collective-permute-start | bytes 1671176 | tf_op jit(solution)/shard_map/ppermute | solution.py:192
  178.6 9.6 %collective-permute-start.21 = (bf16[544,256]{1,0:T(8,128)(2,1)S(1)}, bf16[544,256]{1,0:T(8,128)(2,1)S(1)}, u32[]{:S(2)}, u32[]{:S(2)}) collective-permute-start(bf16[544,256]{1,0:T(8,128)(2,1)S(1)} %collective-permute-done.20), channel_id=1, source_target_pairs={{0,1},{1,0},{8,9},{9,8},{16,17},{17,16},{24,25},{25,24},{2,3},{3,2... | collective-permute-start | bytes 835592 | tf_op jit(solution)/shard_map/ppermute | solution.py:192
  179.5 8.7 %collective-permute-start.22 = (bf16[544,256]{1,0:T(8,128)(2,1)S(1)}, bf16[544,256]{1,0:T(8,128)(2,1)S(1)}, u32[]{:S(2)}, u32[]{:S(2)}) collective-permute-start(bf16[544,256]{1,0:T(8,128)(2,1)S(1)} %collective-permute-done.19), channel_id=1, source_target_pairs={{0,16},{1,17},{8,24},{9,25},{16,0},{17,1},{24,8},{25,9},{2,18},{3,... | collective-permute-start | bytes 835592 | tf_op jit(solution)/shard_map/ppermute | solution.py:192
  180.6 8.2 %collective-permute-start.29 = (bf16[1088,256]{1,0:T(8,128)(2,1)S(1)}, bf16[1088,256]{1,0:T(8,128)(2,1)S(1)}, u32[]{:S(2)}, u32[]{:S(2)}) collective-permute-start(bf16[1088,256]{1,0:T(8,128)(2,1)S(1)} %constant_dynamic-update-slice_fusion.2.refs_3_), channel_id=1, source_target_pairs={{0,8},{1,9},{8,0},{9,1},{16,24},{17,25},{24,16},{25,17},{2,10},{3,... | collective-permute-start | bytes 1671176 | tf_op jit(solution)/shard_map/ppermute | solution.py:192
  180.7 8.1 %collective-permute-start.28 = (bf16[1088,256]{1,0:T(8,128)(2,1)S(1)}, bf16[1088,256]{1,0:T(8,128)(2,1)S(1)}, u32[]{:S(2)}, u32[]{:S(2)}) collective-permute-start(bf16[1088,256]{1,0:T(8,128)(2,1)S(1)} %constant_dynamic-update-slice_fusion.refs_2_), channel_id=1, source_target_pairs={{0,8},{1,9},{8,0},{9,1},{16,24},{17,25},{24,16},{25,17},{2,10},{3,... | collective-permute-start | bytes 1671176 | tf_op jit(solution)/shard_map/ppermute | solution.py:192
  188.2 1.8 collective-permute-start.23
  188.4 1.9 collective-permute-start.24
  196.8 30.4 %all-to-all-start.1 = ((bf16[32,128,128]{2,1,0:T(8,128)(2,1)}), bf16[32,128,128]{2,1,0:T(8,128)(2,1)S(1)}, u32[]{:S(2)}, u32[]{:S(2)}) async-start(bf16[32,128,128]{2,1,0:T(8,128)(2,1)} %get-tuple-element.58), calls=%async_computation.1 | async-start | bytes 2097152 | tf_op jit(solution)/shard_map/all_to_all | solution.py:796

commit v2 on v1

--- a/solution.py
+++ b/solution.py
@@ -58,13 +58,11 @@
         pltpu.make_async_copy(x_ref.at[slot_ref[m]], held.at[m], load_sems.at[m])
         for m in range(mats)
     ]
-    for load in loads[:2]:
+    for load in loads:
         load.start()
     stores = []
     for m in range(mats):
         loads[m].wait()
-        if m + 2 < mats:
-            loads[m + 2].start()
         for g in range(outer):
             for s in range(sub):
                 at = (g * sub + s) * width
@@ -223,8 +221,11 @@
     lower_y = swap(late[1], along_y)
     upper_xy = swap(upper_y, along_x)
     lower_xy = swap(lower_x, along_y)
-    here = [upper, lower, upper_x, lower_x, upper_y, lower_y, upper_xy, lower_xy]
-    return here + [swap(upper, core), lower_core] + [swap(value, core) for value in here[2:]]
+    strips = [upper, lower, swap(upper, core), lower_core, upper_x, lower_x, upper_y, lower_y]
+    full = spread_halves(strips, [0, core, along_x, along_y])
+    rest = [swap(value, core) for value in strips[4:]]
+    far, full = lax.optimization_barrier(((upper_xy, lower_xy), full))
+    return full, [*rest, *far, *[swap(value, core) for value in far]]
 
 
 def gather_second(upper, lower, strip, sub, first_work, second_work):
@@ -316,14 +317,39 @@
         fill_strip(full, strip, member_index() ^ mask, blocks, width)
 
 
+def spread_halves_kernel(places, *refs):
+    full, strip = refs[-2:]
+    fill_halves(full, refs[:-2], places, strip)
+
+
+def spread_halves(halves, places):
+    cut, width = halves[0].shape
+    rows = width * lax.axis_size(team)
+    return pl.pallas_call(
+        functools.partial(spread_halves_kernel, places),
+        in_specs=[ONCHIP] * len(halves),
+        out_specs=ONCHIP,
+        out_shape=pltpu.VMEM((rows, rows), halves[0].dtype),
+        scratch_shapes=[pltpu.VMEM((2 * cut, width), halves[0].dtype)],
+        compiler_params=params(16),
+        cost_estimate=pl.CostEstimate(
+            flops=2 * cut * width * 256 * len(places),
+            bytes_accessed=12 * cut * width * len(places),
+            transcendentals=0,
+        ),
+        name="spread_halves",
+    )(*[in_vmem(half) for half in halves])
+
+
 def polynomial_kernel(chunk, *refs):
-    halves = refs[:-7]
-    full, upper_out, lower_out, out, poly, middle, last = refs[-7:]
+    halves = refs[1:-6]
+    full, upper_out, lower_out, out, poly, middle = refs[-6:]
     rows = full.shape[0]
     packed, width = out.shape
     blocks = rows // width
     half = blocks // 2
-    fill_halves(full, halves, masks(lax.axis_size("sub")), out)
+    _, _, _, both, _, far_x, far_y, far_both = masks(lax.axis_size("sub"))
+    fill_halves(full, halves, [far_x, far_y, both, far_both], out)
     index = member_index()
     mine = block_of(index, width)
 
@@ -351,41 +377,39 @@
             + quintic_weight * dot(full[at, :], middle[...])
         ).astype(poly.dtype)
 
-    pair = 2 * width
-
-    @pl.loop(0, blocks // 4 + 1)
-    def _(j):
-        at = block_of(lax.rem(lax.div(index, 2) + j, blocks // 2), pair)
-        value = linear_weight * middle[at, :].astype(jnp.float32)
-        last[at, :] = (value + dot(full[at, :], poly[...])).astype(last.dtype)
-
+    def last(at, cols):
+        value = linear_weight * middle[at, cols].astype(jnp.float32)
+        return (value + dot(full[at, :], poly[:, cols])).astype(out.dtype)
+
+    every_col = slice(0, width)
     head = head_rows(width)
     tail = head + (half - 1) * width
-    write_head(out, last[mine, :])
+    write_head(out, last(mine, every_col))
     for k in range(1, half):
         at = block_of(lax.rem(index + k, blocks), width)
-        out[head + (k - 1) * width : head + k * width] = last[at, :]
+        out[head + (k - 1) * width : head + k * width] = last(at, every_col)
     other = pl.multiple_of(lax.rem(index + half, blocks) * width, width)
 
     @pl.when(index < half)
     def _():
-        out[tail:] = last[pl.ds(other, width // 2), :]
+        out[tail:] = last(pl.ds(other, width // 2), every_col)
 
     @pl.when(index >= half)
     def _():
-        out[tail:] = last[pl.ds(other, width), width // 2 :].T
+        out[tail:] = last(pl.ds(other, width), slice(width // 2, width)).T
 
     upper_out[...] = out[: packed // 2]
     lower_out[...] = out[packed // 2 :]
 
 
-def polynomial(halves):
+def polynomial(full, halves):
     cut, width = halves[0].shape
-    rows = width * len(halves) // 2
-    dtype = halves[0].dtype
+    rows = full.shape[0]
+    dtype = full.dtype
     return pl.pallas_call(
         functools.partial(polynomial_kernel, 1024),
-        in_specs=[ONCHIP] * len(halves),
+        in_specs=[ONCHIP] * (1 + len(halves)),
+        input_output_aliases={0: 0},
         out_specs=[ONCHIP] * 4,
         out_shape=[
             pltpu.VMEM((rows, rows), dtype),
@@ -393,13 +417,13 @@
             pltpu.VMEM((cut, width), dtype),
             pltpu.VMEM((2 * cut, width), dtype),
         ],
-        scratch_shapes=[pltpu.VMEM((rows, width), dtype)] * 3,
+        scratch_shapes=[pltpu.VMEM((rows, width), dtype)] * 2,
         compiler_params=params(16),
         cost_estimate=pl.CostEstimate(
             flops=8 * rows * rows * width, bytes_accessed=4 * rows * rows, transcendentals=0
         ),
         name="polynomial",
-    )(*[in_vmem(half) for half in halves])
+    )(in_vmem(full), *[in_vmem(half) for half in halves])
 
 
 def columns(cols, first=0):
@@ -804,7 +828,7 @@
     pieces = pack(iterate, slot_of, outer, sub)
     arrived = exchange(pieces.reshape(mats * members, local_rows, col_width))
     current = arrived.reshape(rows, col_width)
-    gram_whole, upper, lower, strip = polynomial(gather_first(*scatter_sum(current, sub), sub))
+    gram_whole, upper, lower, strip = polynomial(*gather_first(*scatter_sum(current, sub), sub))
 
     def first_work():
         return step_start(gram_whole, current)

time: 298 us -> 295 us (0.990)
  transfers between devices with their start and end apart: 31 -> 31, of which waited for: 15 -> 14; matrix products, arithmetic and copies ran while one was open for 0% -> 0% of each run, Pallas kernels for 15% -> 16%
where the time goes in v2:
time: 295 us
  blocking collectives  158 us (54%)
  Pallas kernels  73.9 us (25%)
  waiting for transfers between devices  39.9 us (14%)
  starting transfers between devices  21.2 us (7%)
    all_to_all x2, blocking collectives, exchange(): lax.all_to_all(pieces, every, split_axis=0, concat_axis=0, tiled=True)  158 us
    ppermute x30, waiting for transfers between devices, swap(): return lax.ppermute(value, team, pairs)  37.4 us
    pallas_call x1, Pallas kernels, second_part(): pl.pallas_call(functools.partial(second_part_kernel, local_rows, chunk),...  24.8 us
    ppermute x30, starting transfers between devices, swap(): return lax.ppermute(value, team, pairs)  18.3 us
    pallas_call x1, Pallas kernels, polynomial(): pl.pallas_call(functools.partial(polynomial_kernel, 1024), in_specs=[ONCH...  10.1 us
    pallas_call x1, Pallas kernels, step_start(): pl.pallas_call(functools.partial(product_kernel, 1024), in_specs=[ONCHIP]...  9.35 us
    pallas_call x2, Pallas kernels, gram(): pl.pallas_call(functools.partial(gram_kernel, masks), in_specs=[ONCHIP],...  7.32 us
    pallas_call x1, Pallas kernels, step_end(): pl.pallas_call(functools.partial(mix_kernel, 1024), in_specs=[ONCHIP] * 3...  6.97 us
  transfers between devices with their start and end apart: 31, of which 14 were waited for; matrix products, arithmetic and copies ran while one was open for 0% of the time, Pallas kernels for 16%

profile of v2, /device:TPU:0, one launch (start us, length us, event | category | flops | bytes accessed | tf_op | source)
XLA Modules:
  0.0 294.8 jit_solution(2002098371973908710)
XLA Ops:
  0.0 4.0 %pack.1 = bf16[4,4,2,64,896]{4,3,2,1,0:T(8,128)(2,1)} custom-call(s32[4]{0:T(128)} %slot_ref.1, bf16[4,64,7168]{2,1,0:T(8,128)(2,1)} %x_ref.1), custom_call_target="tpu_custom_call" | custom-call | bytes 7340032 | tf_op jit(solution)/shard_map/pack/pallas_call | solution.py:81
  4.0 91.1 %all_to_all.15 = bf16[32,64,896]{2,1,0:T(8,128)(2,1)S(1)} all-to-all(bf16[32,64,896]{2,1,0:T(8,128)(2,1)} %bitcast.24), channel_id=1, replica_groups=mesh['grp'=4,'plane'=4,'sub'=2] {'grp','plane','sub'}, dimensions={0} | all-to-all | bytes 7340032 | tf_op jit(solution)/shard_map/all_to_all | solution.py:820
  95.1 3.6 %gram.3 = bf16[4,1088,256]{2,1,0:T(8,128)(2,1)S(1)} custom-call(bf16[2048,896]{1,0:T(8,128)(2,1)S(1)} %bitcast.20), custom_call_target="tpu_custom_call" | custom-call | flops 1996488704 | bytes 5898240 | tf_op jit(solution)/shard_map/gram/pallas_call | solution.py:169
  98.7 3.8 %gram.2 = bf16[4,1088,256]{2,1,0:T(8,128)(2,1)S(1)} custom-call(bf16[2048,896]{1,0:T(8,128)(2,1)S(1)} %bitcast.21), custom_call_target="tpu_custom_call" | custom-call | flops 1996488704 | bytes 5898240 | tf_op jit(solution)/shard_map/gram/pallas_call | solution.py:169
  104.3 0.9 collective-permute-start.1
  105.3 13.1 %collective-permute-done.5 = bf16[2,544,256]{2,1,0:T(8,128)(2,1)S(1)} collective-permute-done((bf16[2,544,256]{2,1,0:T(8,128)(2,1)S(1)}, bf16[2,544,256]{2,1,0:T(8,128)(2,1)S(1)}, u32[]{:S(2)}, u32[]{:S(2)}) %collective-permute-start.5) | collective-permute-done | bytes 557088 | tf_op jit(solution)/shard_map/ppermute | solution.py:190
  118.5 0.9 collective-permute-start.6
  119.6 0.9 collective-permute-start.2
  120.5 5.9 %collective-permute-done.6 = bf16[544,256]{1,0:T(8,128)(2,1)S(1)} collective-permute-done((bf16[544,256]{1,0:T(8,128)(2,1)S(1)}, bf16[544,256]{1,0:T(8,128)(2,1)S(1)}, u32[]{:S(2)}, u32[]{:S(2)}) %collective-permute-start.6) | collective-permute-done | bytes 278560 | tf_op jit(solution)/shard_map/ppermute | solution.py:190
  128.2 1.5 collective-permute-start.11
  129.7 1.2 collective-permute-start.12
  130.9 5.3 %collective-permute-done.7.refs_5_ = bf16[544,256]{1,0:T(8,128)(2,1)S(1)} collective-permute-done((bf16[544,256]{1,0:T(8,128)(2,1)S(1)}, bf16[544,256]{1,0:T(8,128)(2,1)S(1)}, u32[]{:S(2)}, u32[]{:S(2)}) %collective-permute-start.7) | collective-permute-done | bytes 278560 | tf_op jit(solution)/shard_map/ppermute | solution.py:190
  137.1 1.2 collective-permute-start.4
  138.3 3.8 %collective-permute-done.11.refs_4_ = bf16[544,256]{1,0:T(8,128)(2,1)S(1)} collective-permute-done((bf16[544,256]{1,0:T(8,128)(2,1)S(1)}, bf16[544,256]{1,0:T(8,128)(2,1)S(1)}, u32[]{:S(2)}, u32[]{:S(2)}) %collective-permute-start.11) | collective-permute-done | bytes 278560 | tf_op jit(solution)/shard_map/ppermute | solution.py:190
  142.1 1.0 collective-permute-done.12.refs_7_
  144.0 4.3 %collective-permute-done.8.refs_6_ = bf16[544,256]{1,0:T(8,128)(2,1)S(1)} collective-permute-done((bf16[544,256]{1,0:T(8,128)(2,1)S(1)}, bf16[544,256]{1,0:T(8,128)(2,1)S(1)}, u32[]{:S(2)}, u32[]{:S(2)}) %collective-permute-start.8) | collective-permute-done | bytes 278560 | tf_op jit(solution)/shard_map/ppermute | solution.py:190
  149.3 0.9 collective-permute-done.13.refs_1_
  151.1 10.1 %polynomial.1 = (bf16[2048,2048]{1,0:T(8,128)(2,1)S(1)}, bf16[544,256]{1,0:T(8,128)(2,1)S(1)}, bf16[544,256]{1,0:T(8,128)(2,1)S(1)}, bf16[1088,256]{1,0:T(8,128)(2,1)S(1)}) custom-call(bf16[2048,2048]{1,0:T(8,128)(2,1)S(1)} %spread_halves.1.refs_0_, bf16[544,256]{1,0:T(8,128)(2,1)S(1)} %collective-permute-done.13.refs_1_, ...), custom_call_target="tpu_custom_call", output_to_operand_aliasing={{0}: (0, {})} | custom-call | flops 8589934592 | bytes 16777216 | tf_op jit(solution)/shard_map/polynomial/pallas_call | solution.py:409
  162.0 1.5 collective-permute-start.19
  164.0 1.3 collective-permute-start.20
  165.3 9.4 %product.1 = (bf16[2048,640]{1,0:T(8,128)(2,1)S(1)}, bf16[2048,2048]{1,0:T(8,128)(2,1)}, bf16[2048,256]{1,0:T(8,128)(2,1)}, bf16[2048,256]{1,0:T(8,128)(2,1)}) custom-call(bf16[2048,2048]{1,0:T(8,128)(2,1)S(1)} %get-tuple-element.46.gram_ref, bf16[2048,896]{1,0:T(8,128)(2,1)S(1)} %bitcast.22), custom_call_target="tpu_custom_call" | custom-call | flops 7516192768 | bytes 16777216 | tf_op jit(solution)/shard_map/product/pallas_call | solution.py:468
  174.7 1.3 collective-permute-done.20
  175.9 1.2 collective-permute-start.21
  177.2 1.1 collective-permute-start.22
  178.9 7.0 %mix.1.refs_5_ = bf16[2048,640]{1,0:T(8,128)(2,1)S(1)} custom-call(bf16[2048,2048]{1,0:T(8,128)(2,1)S(1)} %get-tuple-element.46.gram_ref, bf16[2048,896]{1,0:T(8,128)(2,1)S(1)} %bitcast.23, bf16[2048,640]{1,0:T(8,128)(2,1)S(1)} %get-tuple-element.53.product_ref), custom_call_target="tpu_custom_call" | custom-call | flops 5368709120 | bytes 8388608 | tf_op jit(solution)/shard_map/mix/pallas_call | solution.py:500
  186.5 1.2 spread.1.refs_4_
  187.9 6.6 %first_part.1 = (bf16[2048,2048]{1,0:T(8,128)(2,1)S(1)}, bf16[2048,2048]{1,0:T(8,128)(2,1)}, bf16[2048,384]{1,0:T(8,128)(2,1)}, bf16[32,128,128]{2,1,0:T(8,128)(2,1)}, f32[1,256]{1,0:T(1,128)S(1)}) custom-call(bf16[544,256]{1,0:T(8,128)(2,1)S(1)} %collective-permute-done.21.refs_0_, ...), custom_call_target="tpu_custom_call", output_to_operand_aliasing={{0}: (4, {})} | custom-call | flops 4294967296 | bytes 16777216 | tf_op jit(solution)/shard_map/first_part/pallas_call | solution.py:574
  194.5 2.9 all-to-all-start.1
  197.4 24.8 %second_part.1 = bf16[32,336,128]{2,1,0:T(8,128)(2,1)} custom-call(bf16[2048,2048]{1,0:T(8,128)(2,1)} %get-tuple-element.65.before_hbm, bf16[2048,256]{1,0:T(8,128)(2,1)} %get-tuple-element.66.late_hbm, bf16[2048,256]{1,0:T(8,128)(2,1)} %get-tuple-element.67.late_product_hbm, bf16[2048,2048]{1,0:T(8,128)(2,1)} %get-tuple-element.68.gram_hbm, ...), custom_call_target="tpu_custom_call" | custom-call | flops 15032385536 | bytes 33554432 | tf_op jit(solution)/shard_map/second_part/pallas_call | solution.py:720
  222.3 2.5 all-to-all-done.1
  224.8 67.2 %all_to_all.16 = bf16[32,336,128]{2,1,0:T(8,128)(2,1)S(1)} all-to-all(bf16[32,336,128]{2,1,0:T(8,128)(2,1)} %second_part.1), channel_id=1, replica_groups=mesh['grp'=4,'plane'=4,'sub'=2] {'grp','plane','sub'}, dimensions={0} | all-to-all | bytes 5505024 | tf_op jit(solution)/shard_map/all_to_all | solution.py:820
  292.0 2.8 scaled.1
  (57 shorter events, 10.4 us)
Async XLA Ops:
  98.6 4.4 %collective-permute-start = (bf16[4,1088,256]{2,1,0:T(8,128)(2,1)S(1)}, bf16[4,1088,256]{2,1,0:T(8,128)(2,1)S(1)}, u32[]{:S(2)}, u32[]{:S(2)}) collective-permute-start(bf16[4,1088,256]{2,1,0:T(8,128)(2,1)S(1)} %gram.3), channel_id=1, source_target_pairs={{0,8},{1,9},{8,0},{9,1},{16,24},{17,25},{24,16},{25,17},{2,10},{3,... | collective-permute-start | bytes 6684680 | tf_op jit(solution)/shard_map/ppermute | solution.py:190
  103.6 14.7 %collective-permute-start.5 = (bf16[2,544,256]{2,1,0:T(8,128)(2,1)S(1)}, bf16[2,544,256]{2,1,0:T(8,128)(2,1)S(1)}, u32[]{:S(2)}, u32[]{:S(2)}) collective-permute-start(bf16[2,544,256]{2,1,0:T(8,128)(2,1)S(1)} %slice.43), channel_id=1, source_target_pairs={{0,16},{1,17},{8,24},{9,25},{16,0},{17,1},{24,8},{25,9},{2,18},{3,... | collective-permute-start | bytes 1671176 | tf_op jit(solution)/shard_map/ppermute | solution.py:190
  104.3 15.1 %collective-permute-start.1 = (bf16[2,544,256]{2,1,0:T(8,128)(2,1)S(1)}, bf16[2,544,256]{2,1,0:T(8,128)(2,1)S(1)}, u32[]{:S(2)}, u32[]{:S(2)}) collective-permute-start(bf16[2,544,256]{2,1,0:T(8,128)(2,1)S(1)} %slice.32), channel_id=1, source_target_pairs={{0,1},{1,0},{8,9},{9,8},{16,17},{17,16},{24,25},{25,24},{2,3},{3,2... | collective-permute-start | bytes 1671176 | tf_op jit(solution)/shard_map/ppermute | solution.py:190
  118.5 7.9 %collective-permute-start.6 = (bf16[544,256]{1,0:T(8,128)(2,1)S(1)}, bf16[544,256]{1,0:T(8,128)(2,1)S(1)}, u32[]{:S(2)}, u32[]{:S(2)}) collective-permute-start(bf16[544,256]{1,0:T(8,128)(2,1)S(1)} %slice_bitcast_fusion), channel_id=1, source_target_pairs={{0,1},{1,0},{8,9},{9,8},{16,17},{17,16},{24,25},{25,24},{2,3},{3,2... | collective-permute-start | bytes 835592 | tf_op jit(solution)/shard_map/ppermute | solution.py:190
  119.6 7.9 %collective-permute-start.2 = (bf16[544,256]{1,0:T(8,128)(2,1)S(1)}, bf16[544,256]{1,0:T(8,128)(2,1)S(1)}, u32[]{:S(2)}, u32[]{:S(2)}) collective-permute-start(bf16[544,256]{1,0:T(8,128)(2,1)S(1)} %slice_bitcast_fusion.2), channel_id=1, source_target_pairs={{0,16},{1,17},{8,24},{9,25},{16,0},{17,1},{24,8},{25,9},{2,18},{3,... | collective-permute-start | bytes 835592 | tf_op jit(solution)/shard_map/ppermute | solution.py:190
  126.5 1.7 collective-permute-start.10
  126.6 9.5 %collective-permute-start.7 = (bf16[544,256]{1,0:T(8,128)(2,1)S(1)}, bf16[544,256]{1,0:T(8,128)(2,1)S(1)}, u32[]{:S(2)}, u32[]{:S(2)}) collective-permute-start(bf16[544,256]{1,0:T(8,128)(2,1)S(1)} %fusion.refs_1_), channel_id=1, source_target_pairs={{0,1},{1,0},{8,9},{9,8},{16,17},{17,16},{24,25},{25,24},{2,3},{3,2... | collective-permute-start | bytes 835592 | tf_op jit(solution)/shard_map/ppermute | solution.py:190
  127.6 9.6 %collective-permute-start.3 = (bf16[544,256]{1,0:T(8,128)(2,1)S(1)}, bf16[544,256]{1,0:T(8,128)(2,1)S(1)}, u32[]{:S(2)}, u32[]{:S(2)}) collective-permute-start(bf16[544,256]{1,0:T(8,128)(2,1)S(1)} %fusion.1.refs_0_), channel_id=1, source_target_pairs={{0,16},{1,17},{8,24},{9,25},{16,0},{17,1},{24,8},{25,9},{2,18},{3,... | collective-permute-start | bytes 835592 | tf_op jit(solution)/shard_map/ppermute | solution.py:190
  128.2 10.1 %collective-permute-start.9 = (bf16[544,256]{1,0:T(8,128)(2,1)S(1)}, bf16[544,256]{1,0:T(8,128)(2,1)S(1)}, u32[]{:S(2)}, u32[]{:S(2)}) collective-permute-start(bf16[544,256]{1,0:T(8,128)(2,1)S(1)} %fusion.1.refs_0_), channel_id=1, source_target_pairs={{0,8},{1,9},{8,0},{9,1},{16,24},{17,25},{24,16},{25,17},{2,10},{3,... | collective-permute-start | bytes 835592 | tf_op jit(solution)/shard_map/ppermute | solution.py:190
  128.2 13.9 %collective-permute-start.11 = (bf16[544,256]{1,0:T(8,128)(2,1)S(1)}, bf16[544,256]{1,0:T(8,128)(2,1)S(1)}, u32[]{:S(2)}, u32[]{:S(2)}) collective-permute-start(bf16[544,256]{1,0:T(8,128)(2,1)S(1)} %fusion.1.refs_0_), channel_id=1, source_target_pairs={{0,1},{1,0},{8,9},{9,8},{16,17},{17,16},{24,25},{25,24},{2,3},{3,2... | collective-permute-start | bytes 835592 | tf_op jit(solution)/shard_map/ppermute | solution.py:190
  129.7 13.4 %collective-permute-start.12 = (bf16[544,256]{1,0:T(8,128)(2,1)S(1)}, bf16[544,256]{1,0:T(8,128)(2,1)S(1)}, u32[]{:S(2)}, u32[]{:S(2)}) collective-permute-start(bf16[544,256]{1,0:T(8,128)(2,1)S(1)} %fusion.refs_1_), channel_id=1, source_target_pairs={{0,16},{1,17},{8,24},{9,25},{16,0},{17,1},{24,8},{25,9},{2,18},{3,... | collective-permute-start | bytes 835592 | tf_op jit(solution)/shard_map/ppermute | solution.py:190
  136.1 12.2 %collective-permute-start.8 = (bf16[544,256]{1,0:T(8,128)(2,1)S(1)}, bf16[544,256]{1,0:T(8,128)(2,1)S(1)}, u32[]{:S(2)}, u32[]{:S(2)}) collective-permute-start(bf16[544,256]{1,0:T(8,128)(2,1)S(1)} %collective-permute-done.7.refs_5_), channel_id=1, source_target_pairs={{0,16},{1,17},{8,24},{9,25},{16,0},{17,1},{24,8},{25,9},{2,18},{3,... | collective-permute-start | bytes 835592 | tf_op jit(solution)/shard_map/ppermute | solution.py:190
  137.1 11.2 %collective-permute-start.4 = (bf16[544,256]{1,0:T(8,128)(2,1)S(1)}, bf16[544,256]{1,0:T(8,128)(2,1)S(1)}, u32[]{:S(2)}, u32[]{:S(2)}) collective-permute-start(bf16[544,256]{1,0:T(8,128)(2,1)S(1)} %collective-permute-done.3.refs_6_), channel_id=1, source_target_pairs={{0,1},{1,0},{8,9},{9,8},{16,17},{17,16},{24,25},{25,24},{2,3},{3,2... | collective-permute-start | bytes 835592 | tf_op jit(solution)/shard_map/ppermute | solution.py:190
  138.3 10.5 %collective-permute-start.14 = (bf16[544,256]{1,0:T(8,128)(2,1)S(1)}, bf16[544,256]{1,0:T(8,128)(2,1)S(1)}, u32[]{:S(2)}, u32[]{:S(2)}) collective-permute-start(bf16[544,256]{1,0:T(8,128)(2,1)S(1)} %collective-permute-done.7.refs_5_), channel_id=1, source_target_pairs={{0,8},{1,9},{8,0},{9,1},{16,24},{17,25},{24,16},{25,17},{2,10},{3,... | collective-permute-start | bytes 835592 | tf_op jit(solution)/shard_map/ppermute | solution.py:190
  142.1 7.3 %collective-permute-start.15 = (bf16[544,256]{1,0:T(8,128)(2,1)S(1)}, bf16[544,256]{1,0:T(8,128)(2,1)S(1)}, u32[]{:S(2)}, u32[]{:S(2)}) collective-permute-start(bf16[544,256]{1,0:T(8,128)(2,1)S(1)} %collective-permute-done.3.refs_6_), channel_id=1, source_target_pairs={{0,8},{1,9},{8,0},{9,1},{16,24},{17,25},{24,16},{25,17},{2,10},{3,... | collective-permute-start | bytes 835592 | tf_op jit(solution)/shard_map/ppermute | solution.py:190
  148.3 2.4 collective-permute-start.17
  148.3 2.0 collective-permute-start.13
  148.8 1.8 collective-permute-start.16
  148.8 2.2 collective-permute-start.18
  161.2 17.1 %collective-permute-start.27 = (bf16[544,256]{1,0:T(8,128)(2,1)S(1)}, bf16[544,256]{1,0:T(8,128)(2,1)S(1)}, u32[]{:S(2)}, u32[]{:S(2)}) collective-permute-start(bf16[544,256]{1,0:T(8,128)(2,1)S(1)} %get-tuple-element.44), channel_id=1, source_target_pairs={{0,16},{1,17},{8,24},{9,25},{16,0},{17,1},{24,8},{25,9},{2,18},{3,... | collective-permute-start | bytes 835592 | tf_op jit(solution)/shard_map/ppermute | solution.py:190
  162.0 12.7 %collective-permute-start.19 = (bf16[544,256]{1,0:T(8,128)(2,1)S(1)}, bf16[544,256]{1,0:T(8,128)(2,1)S(1)}, u32[]{:S(2)}, u32[]{:S(2)}) collective-permute-start(bf16[544,256]{1,0:T(8,128)(2,1)S(1)} %get-tuple-element.44), channel_id=1, source_target_pairs={{0,1},{1,0},{8,9},{9,8},{16,17},{17,16},{24,25},{25,24},{2,3},{3,2... | collective-permute-start | bytes 835592 | tf_op jit(solution)/shard_map/ppermute | solution.py:190
  163.5 14.8 %collective-permute-start.26 = (bf16[544,256]{1,0:T(8,128)(2,1)S(1)}, bf16[544,256]{1,0:T(8,128)(2,1)S(1)}, u32[]{:S(2)}, u32[]{:S(2)}) collective-permute-start(bf16[544,256]{1,0:T(8,128)(2,1)S(1)} %get-tuple-element.45), channel_id=1, source_target_pairs={{0,1},{1,0},{8,9},{9,8},{16,17},{17,16},{24,25},{25,24},{2,3},{3,2... | collective-permute-start | bytes 835592 | tf_op jit(solution)/shard_map/ppermute | solution.py:190
  164.0 12.0 %collective-permute-start.20 = (bf16[544,256]{1,0:T(8,128)(2,1)S(1)}, bf16[544,256]{1,0:T(8,128)(2,1)S(1)}, u32[]{:S(2)}, u32[]{:S(2)}) collective-permute-start(bf16[544,256]{1,0:T(8,128)(2,1)S(1)} %get-tuple-element.45), channel_id=1, source_target_pairs={{0,16},{1,17},{8,24},{9,25},{16,0},{17,1},{24,8},{25,9},{2,18},{3,... | collective-permute-start | bytes 835592 | tf_op jit(solution)/shard_map/ppermute | solution.py:190
  165.3 21.2 %collective-permute-start.25 = (bf16[1088,256]{1,0:T(8,128)(2,1)S(1)}, bf16[1088,256]{1,0:T(8,128)(2,1)S(1)}, u32[]{:S(2)}, u32[]{:S(2)}) collective-permute-start(bf16[1088,256]{1,0:T(8,128)(2,1)S(1)} %get-tuple-element.59.refs_0_), channel_id=1, source_target_pairs={{0,8},{1,9},{8,0},{9,1},{16,24},{17,25},{24,16},{25,17},{2,10},{3,... | collective-permute-start | bytes 1671176 | tf_op jit(solution)/shard_map/ppermute | solution.py:190
  175.9 10.0 %collective-permute-start.21 = (bf16[544,256]{1,0:T(8,128)(2,1)S(1)}, bf16[544,256]{1,0:T(8,128)(2,1)S(1)}, u32[]{:S(2)}, u32[]{:S(2)}) collective-permute-start(bf16[544,256]{1,0:T(8,128)(2,1)S(1)} %collective-permute-done.20), channel_id=1, source_target_pairs={{0,1},{1,0},{8,9},{9,8},{16,17},{17,16},{24,25},{25,24},{2,3},{3,2... | collective-permute-start | bytes 835592 | tf_op jit(solution)/shard_map/ppermute | solution.py:190
  177.2 8.8 %collective-permute-start.22 = (bf16[544,256]{1,0:T(8,128)(2,1)S(1)}, bf16[544,256]{1,0:T(8,128)(2,1)S(1)}, u32[]{:S(2)}, u32[]{:S(2)}) collective-permute-start(bf16[544,256]{1,0:T(8,128)(2,1)S(1)} %collective-permute-done.19), channel_id=1, source_target_pairs={{0,16},{1,17},{8,24},{9,25},{16,0},{17,1},{24,8},{25,9},{2,18},{3,... | collective-permute-start | bytes 835592 | tf_op jit(solution)/shard_map/ppermute | solution.py:190
  178.3 8.2 %collective-permute-start.29 = (bf16[1088,256]{1,0:T(8,128)(2,1)S(1)}, bf16[1088,256]{1,0:T(8,128)(2,1)S(1)}, u32[]{:S(2)}, u32[]{:S(2)}) collective-permute-start(bf16[1088,256]{1,0:T(8,128)(2,1)S(1)} %constant_dynamic-update-slice_fusion.2.refs_3_), channel_id=1, source_target_pairs={{0,8},{1,9},{8,0},{9,1},{16,24},{17,25},{24,16},{25,17},{2,10},{3,... | collective-permute-start | bytes 1671176 | tf_op jit(solution)/shard_map/ppermute | solution.py:190
  178.4 8.1 %collective-permute-start.28 = (bf16[1088,256]{1,0:T(8,128)(2,1)S(1)}, bf16[1088,256]{1,0:T(8,128)(2,1)S(1)}, u32[]{:S(2)}, u32[]{:S(2)}) collective-permute-start(bf16[1088,256]{1,0:T(8,128)(2,1)S(1)} %constant_dynamic-update-slice_fusion.refs_2_), channel_id=1, source_target_pairs={{0,8},{1,9},{8,0},{9,1},{16,24},{17,25},{24,16},{25,17},{2,10},{3,... | collective-permute-start | bytes 1671176 | tf_op jit(solution)/shard_map/ppermute | solution.py:190
  185.9 1.8 collective-permute-start.23
  186.1 1.9 collective-permute-start.24
  194.5 30.3 %all-to-all-start.1 = ((bf16[32,128,128]{2,1,0:T(8,128)(2,1)}), bf16[32,128,128]{2,1,0:T(8,128)(2,1)S(1)}, u32[]{:S(2)}, u32[]{:S(2)}) async-start(bf16[32,128,128]{2,1,0:T(8,128)(2,1)} %get-tuple-element.64), calls=%async_computation.1 | async-start | bytes 2097152 | tf_op jit(solution)/shard_map/all_to_all | solution.py:820

commit v3 on v2

--- a/solution.py
+++ b/solution.py
@@ -55,14 +55,18 @@
 def pack_kernel(slot_ref, x_ref, o_ref, held, load_sems, store_sems):
     outer, mats, sub, _, width = o_ref.shape
     loads = [
-        pltpu.make_async_copy(x_ref.at[slot_ref[m]], held.at[m], load_sems.at[m])
+        pltpu.make_async_copy(
+            x_ref.at[slot_ref[m], rows], held.at[m, rows], load_sems.at[2 * m + i]
+        )
         for m in range(mats)
+        for i, rows in enumerate((slice(0, held.shape[1] // 2), slice(held.shape[1] // 2, None)))
     ]
     for load in loads:
         load.start()
     stores = []
     for m in range(mats):
-        loads[m].wait()
+        loads[2 * m].wait()
+        loads[2 * m + 1].wait()
         for g in range(outer):
             for s in range(sub):
                 at = (g * sub + s) * width
@@ -87,7 +91,7 @@
             out_specs=HBM,
             scratch_shapes=[
                 pltpu.VMEM(iterate.shape, iterate.dtype),
-                pltpu.SemaphoreType.DMA((mats,)),
+                pltpu.SemaphoreType.DMA((2 * mats,)),
                 pltpu.SemaphoreType.DMA((mats * outer * sub,)),
             ],
         ),

time: 295 us -> 295 us (level)
  no operation moved by 1% of the time
where the time goes in v3:
time: 295 us
  blocking collectives  158 us (54%)
  Pallas kernels  73.9 us (25%)
  waiting for transfers between devices  39.9 us (14%)
  starting transfers between devices  21.2 us (7%)
    all_to_all x2, blocking collectives, exchange(): lax.all_to_all(pieces, every, split_axis=0, concat_axis=0, tiled=True)  158 us
    ppermute x30, waiting for transfers between devices, swap(): return lax.ppermute(value, team, pairs)  37.4 us
    pallas_call x1, Pallas kernels, second_part(): pl.pallas_call(functools.partial(second_part_kernel, local_rows, chunk),...  24.8 us
    ppermute x30, starting transfers between devices, swap(): return lax.ppermute(value, team, pairs)  18.3 us
    pallas_call x1, Pallas kernels, polynomial(): pl.pallas_call(functools.partial(polynomial_kernel, 1024), in_specs=[ONCH...  10.1 us
    pallas_call x1, Pallas kernels, step_start(): pl.pallas_call(functools.partial(product_kernel, 1024), in_specs=[ONCHIP]...  9.35 us
    pallas_call x2, Pallas kernels, gram(): pl.pallas_call(functools.partial(gram_kernel, masks), in_specs=[ONCHIP],...  7.31 us
    pallas_call x1, Pallas kernels, step_end(): pl.pallas_call(functools.partial(mix_kernel, 1024), in_specs=[ONCHIP] * 3...  6.97 us
  transfers between devices with their start and end apart: 31, of which 14 were waited for; matrix products, arithmetic and copies ran while one was open for 0% of the time, Pallas kernels for 16%

profile of v3, /device:TPU:0, one launch (start us, length us, event | category | flops | bytes accessed | tf_op | source)
XLA Modules:
  0.0 294.8 jit_solution(1416762101246197554)
XLA Ops:
  0.0 4.0 %pack.1 = bf16[4,4,2,64,896]{4,3,2,1,0:T(8,128)(2,1)} custom-call(s32[4]{0:T(128)} %slot_ref.1, bf16[4,64,7168]{2,1,0:T(8,128)(2,1)} %x_ref.1), custom_call_target="tpu_custom_call" | custom-call | bytes 7340032 | tf_op jit(solution)/shard_map/pack/pallas_call | solution.py:85
  4.0 91.1 %all_to_all.15 = bf16[32,64,896]{2,1,0:T(8,128)(2,1)S(1)} all-to-all(bf16[32,64,896]{2,1,0:T(8,128)(2,1)} %bitcast.24), channel_id=1, replica_groups=mesh['grp'=4,'plane'=4,'sub'=2] {'grp','plane','sub'}, dimensions={0} | all-to-all | bytes 7340032 | tf_op jit(solution)/shard_map/all_to_all | solution.py:824
  95.1 3.6 %gram.3 = bf16[4,1088,256]{2,1,0:T(8,128)(2,1)S(1)} custom-call(bf16[2048,896]{1,0:T(8,128)(2,1)S(1)} %bitcast.20), custom_call_target="tpu_custom_call" | custom-call | flops 1996488704 | bytes 5898240 | tf_op jit(solution)/shard_map/gram/pallas_call | solution.py:173
  98.7 3.7 %gram.2 = bf16[4,1088,256]{2,1,0:T(8,128)(2,1)S(1)} custom-call(bf16[2048,896]{1,0:T(8,128)(2,1)S(1)} %bitcast.21), custom_call_target="tpu_custom_call" | custom-call | flops 1996488704 | bytes 5898240 | tf_op jit(solution)/shard_map/gram/pallas_call | solution.py:173
  105.2 13.1 %collective-permute-done.5 = bf16[2,544,256]{2,1,0:T(8,128)(2,1)S(1)} collective-permute-done((bf16[2,544,256]{2,1,0:T(8,128)(2,1)S(1)}, bf16[2,544,256]{2,1,0:T(8,128)(2,1)S(1)}, u32[]{:S(2)}, u32[]{:S(2)}) %collective-permute-start.5) | collective-permute-done | bytes 557088 | tf_op jit(solution)/shard_map/ppermute | solution.py:194
  118.5 0.9 collective-permute-start.6
  119.6 0.9 collective-permute-start.2
  120.5 5.9 %collective-permute-done.6 = bf16[544,256]{1,0:T(8,128)(2,1)S(1)} collective-permute-done((bf16[544,256]{1,0:T(8,128)(2,1)S(1)}, bf16[544,256]{1,0:T(8,128)(2,1)S(1)}, u32[]{:S(2)}, u32[]{:S(2)}) %collective-permute-start.6) | collective-permute-done | bytes 278560 | tf_op jit(solution)/shard_map/ppermute | solution.py:194
  126.6 0.9 collective-permute-start.7
  128.2 1.5 collective-permute-start.11
  129.7 1.1 collective-permute-start.12
  130.9 5.3 %collective-permute-done.7.refs_5_ = bf16[544,256]{1,0:T(8,128)(2,1)S(1)} collective-permute-done((bf16[544,256]{1,0:T(8,128)(2,1)S(1)}, bf16[544,256]{1,0:T(8,128)(2,1)S(1)}, u32[]{:S(2)}, u32[]{:S(2)}) %collective-permute-start.7) | collective-permute-done | bytes 278560 | tf_op jit(solution)/shard_map/ppermute | solution.py:194
  137.2 1.2 collective-permute-start.4
  138.3 3.8 %collective-permute-done.11.refs_4_ = bf16[544,256]{1,0:T(8,128)(2,1)S(1)} collective-permute-done((bf16[544,256]{1,0:T(8,128)(2,1)S(1)}, bf16[544,256]{1,0:T(8,128)(2,1)S(1)}, u32[]{:S(2)}, u32[]{:S(2)}) %collective-permute-start.11) | collective-permute-done | bytes 278560 | tf_op jit(solution)/shard_map/ppermute | solution.py:194
  142.1 1.0 collective-permute-done.12.refs_7_
  144.0 4.3 %collective-permute-done.8.refs_6_ = bf16[544,256]{1,0:T(8,128)(2,1)S(1)} collective-permute-done((bf16[544,256]{1,0:T(8,128)(2,1)S(1)}, bf16[544,256]{1,0:T(8,128)(2,1)S(1)}, u32[]{:S(2)}, u32[]{:S(2)}) %collective-permute-start.8) | collective-permute-done | bytes 278560 | tf_op jit(solution)/shard_map/ppermute | solution.py:194
  149.4 0.9 collective-permute-done.13.refs_1_
  151.1 10.1 %polynomial.1 = (bf16[2048,2048]{1,0:T(8,128)(2,1)S(1)}, bf16[544,256]{1,0:T(8,128)(2,1)S(1)}, bf16[544,256]{1,0:T(8,128)(2,1)S(1)}, bf16[1088,256]{1,0:T(8,128)(2,1)S(1)}) custom-call(bf16[2048,2048]{1,0:T(8,128)(2,1)S(1)} %spread_halves.1.refs_0_, bf16[544,256]{1,0:T(8,128)(2,1)S(1)} %collective-permute-done.13.refs_1_, ...), custom_call_target="tpu_custom_call", output_to_operand_aliasing={{0}: (0, {})} | custom-call | flops 8589934592 | bytes 16777216 | tf_op jit(solution)/shard_map/polynomial/pallas_call | solution.py:413
  161.9 1.6 collective-permute-start.19
  163.9 1.4 collective-permute-start.20
  165.3 9.4 %product.1 = (bf16[2048,640]{1,0:T(8,128)(2,1)S(1)}, bf16[2048,2048]{1,0:T(8,128)(2,1)}, bf16[2048,256]{1,0:T(8,128)(2,1)}, bf16[2048,256]{1,0:T(8,128)(2,1)}) custom-call(bf16[2048,2048]{1,0:T(8,128)(2,1)S(1)} %get-tuple-element.46.gram_ref, bf16[2048,896]{1,0:T(8,128)(2,1)S(1)} %bitcast.22), custom_call_target="tpu_custom_call" | custom-call | flops 7516192768 | bytes 16777216 | tf_op jit(solution)/shard_map/product/pallas_call | solution.py:472
  174.7 1.3 collective-permute-done.20
  175.9 1.2 collective-permute-start.21
  177.2 1.1 collective-permute-start.22
  178.9 7.0 %mix.1.refs_5_ = bf16[2048,640]{1,0:T(8,128)(2,1)S(1)} custom-call(bf16[2048,2048]{1,0:T(8,128)(2,1)S(1)} %get-tuple-element.46.gram_ref, bf16[2048,896]{1,0:T(8,128)(2,1)S(1)} %bitcast.23, bf16[2048,640]{1,0:T(8,128)(2,1)S(1)} %get-tuple-element.53.product_ref), custom_call_target="tpu_custom_call" | custom-call | flops 5368709120 | bytes 8388608 | tf_op jit(solution)/shard_map/mix/pallas_call | solution.py:504
  186.5 1.2 spread.1.refs_4_
  188.0 6.6 %first_part.1 = (bf16[2048,2048]{1,0:T(8,128)(2,1)S(1)}, bf16[2048,2048]{1,0:T(8,128)(2,1)}, bf16[2048,384]{1,0:T(8,128)(2,1)}, bf16[32,128,128]{2,1,0:T(8,128)(2,1)}, f32[1,256]{1,0:T(1,128)S(1)}) custom-call(bf16[544,256]{1,0:T(8,128)(2,1)S(1)} %collective-permute-done.21.refs_0_, ...), custom_call_target="tpu_custom_call", output_to_operand_aliasing={{0}: (4, {})} | custom-call | flops 4294967296 | bytes 16777216 | tf_op jit(solution)/shard_map/first_part/pallas_call | solution.py:578
  194.5 2.9 all-to-all-start.1
  197.5 24.8 %second_part.1 = bf16[32,336,128]{2,1,0:T(8,128)(2,1)} custom-call(bf16[2048,2048]{1,0:T(8,128)(2,1)} %get-tuple-element.65.before_hbm, bf16[2048,256]{1,0:T(8,128)(2,1)} %get-tuple-element.66.late_hbm, bf16[2048,256]{1,0:T(8,128)(2,1)} %get-tuple-element.67.late_product_hbm, bf16[2048,2048]{1,0:T(8,128)(2,1)} %get-tuple-element.68.gram_hbm, ...), custom_call_target="tpu_custom_call" | custom-call | flops 15032385536 | bytes 33554432 | tf_op jit(solution)/shard_map/second_part/pallas_call | solution.py:724
  222.3 2.5 all-to-all-done.1
  224.8 67.2 %all_to_all.16 = bf16[32,336,128]{2,1,0:T(8,128)(2,1)S(1)} all-to-all(bf16[32,336,128]{2,1,0:T(8,128)(2,1)} %second_part.1), channel_id=1, replica_groups=mesh['grp'=4,'plane'=4,'sub'=2] {'grp','plane','sub'}, dimensions={0} | all-to-all | bytes 5505024 | tf_op jit(solution)/shard_map/all_to_all | solution.py:824
  292.0 2.8 scaled.1
  (57 shorter events, 10.3 us)
Async XLA Ops:
  98.6 4.4 %collective-permute-start = (bf16[4,1088,256]{2,1,0:T(8,128)(2,1)S(1)}, bf16[4,1088,256]{2,1,0:T(8,128)(2,1)S(1)}, u32[]{:S(2)}, u32[]{:S(2)}) collective-permute-start(bf16[4,1088,256]{2,1,0:T(8,128)(2,1)S(1)} %gram.3), channel_id=1, source_target_pairs={{0,8},{1,9},{8,0},{9,1},{16,24},{17,25},{24,16},{25,17},{2,10},{3,... | collective-permute-start | bytes 6684680 | tf_op jit(solution)/shard_map/ppermute | solution.py:194
  103.6 14.7 %collective-permute-start.5 = (bf16[2,544,256]{2,1,0:T(8,128)(2,1)S(1)}, bf16[2,544,256]{2,1,0:T(8,128)(2,1)S(1)}, u32[]{:S(2)}, u32[]{:S(2)}) collective-permute-start(bf16[2,544,256]{2,1,0:T(8,128)(2,1)S(1)} %slice.43), channel_id=1, source_target_pairs={{0,16},{1,17},{8,24},{9,25},{16,0},{17,1},{24,8},{25,9},{2,18},{3,... | collective-permute-start | bytes 1671176 | tf_op jit(solution)/shard_map/ppermute | solution.py:194
  104.3 15.1 %collective-permute-start.1 = (bf16[2,544,256]{2,1,0:T(8,128)(2,1)S(1)}, bf16[2,544,256]{2,1,0:T(8,128)(2,1)S(1)}, u32[]{:S(2)}, u32[]{:S(2)}) collective-permute-start(bf16[2,544,256]{2,1,0:T(8,128)(2,1)S(1)} %slice.32), channel_id=1, source_target_pairs={{0,1},{1,0},{8,9},{9,8},{16,17},{17,16},{24,25},{25,24},{2,3},{3,2... | collective-permute-start | bytes 1671176 | tf_op jit(solution)/shard_map/ppermute | solution.py:194
  118.5 7.9 %collective-permute-start.6 = (bf16[544,256]{1,0:T(8,128)(2,1)S(1)}, bf16[544,256]{1,0:T(8,128)(2,1)S(1)}, u32[]{:S(2)}, u32[]{:S(2)}) collective-permute-start(bf16[544,256]{1,0:T(8,128)(2,1)S(1)} %slice_bitcast_fusion), channel_id=1, source_target_pairs={{0,1},{1,0},{8,9},{9,8},{16,17},{17,16},{24,25},{25,24},{2,3},{3,2... | collective-permute-start | bytes 835592 | tf_op jit(solution)/shard_map/ppermute | solution.py:194
  119.6 7.9 %collective-permute-start.2 = (bf16[544,256]{1,0:T(8,128)(2,1)S(1)}, bf16[544,256]{1,0:T(8,128)(2,1)S(1)}, u32[]{:S(2)}, u32[]{:S(2)}) collective-permute-start(bf16[544,256]{1,0:T(8,128)(2,1)S(1)} %slice_bitcast_fusion.2), channel_id=1, source_target_pairs={{0,16},{1,17},{8,24},{9,25},{16,0},{17,1},{24,8},{25,9},{2,18},{3,... | collective-permute-start | bytes 835592 | tf_op jit(solution)/shard_map/ppermute | solution.py:194
  126.5 1.7 collective-permute-start.10
  126.6 9.5 %collective-permute-start.7 = (bf16[544,256]{1,0:T(8,128)(2,1)S(1)}, bf16[544,256]{1,0:T(8,128)(2,1)S(1)}, u32[]{:S(2)}, u32[]{:S(2)}) collective-permute-start(bf16[544,256]{1,0:T(8,128)(2,1)S(1)} %fusion.refs_1_), channel_id=1, source_target_pairs={{0,1},{1,0},{8,9},{9,8},{16,17},{17,16},{24,25},{25,24},{2,3},{3,2... | collective-permute-start | bytes 835592 | tf_op jit(solution)/shard_map/ppermute | solution.py:194
  127.6 9.6 %collective-permute-start.3 = (bf16[544,256]{1,0:T(8,128)(2,1)S(1)}, bf16[544,256]{1,0:T(8,128)(2,1)S(1)}, u32[]{:S(2)}, u32[]{:S(2)}) collective-permute-start(bf16[544,256]{1,0:T(8,128)(2,1)S(1)} %fusion.1.refs_0_), channel_id=1, source_target_pairs={{0,16},{1,17},{8,24},{9,25},{16,0},{17,1},{24,8},{25,9},{2,18},{3,... | collective-permute-start | bytes 835592 | tf_op jit(solution)/shard_map/ppermute | solution.py:194
  128.2 10.1 %collective-permute-start.9 = (bf16[544,256]{1,0:T(8,128)(2,1)S(1)}, bf16[544,256]{1,0:T(8,128)(2,1)S(1)}, u32[]{:S(2)}, u32[]{:S(2)}) collective-permute-start(bf16[544,256]{1,0:T(8,128)(2,1)S(1)} %fusion.1.refs_0_), channel_id=1, source_target_pairs={{0,8},{1,9},{8,0},{9,1},{16,24},{17,25},{24,16},{25,17},{2,10},{3,... | collective-permute-start | bytes 835592 | tf_op jit(solution)/shard_map/ppermute | solution.py:194
  128.2 13.9 %collective-permute-start.11 = (bf16[544,256]{1,0:T(8,128)(2,1)S(1)}, bf16[544,256]{1,0:T(8,128)(2,1)S(1)}, u32[]{:S(2)}, u32[]{:S(2)}) collective-permute-start(bf16[544,256]{1,0:T(8,128)(2,1)S(1)} %fusion.1.refs_0_), channel_id=1, source_target_pairs={{0,1},{1,0},{8,9},{9,8},{16,17},{17,16},{24,25},{25,24},{2,3},{3,2... | collective-permute-start | bytes 835592 | tf_op jit(solution)/shard_map/ppermute | solution.py:194
  129.7 13.4 %collective-permute-start.12 = (bf16[544,256]{1,0:T(8,128)(2,1)S(1)}, bf16[544,256]{1,0:T(8,128)(2,1)S(1)}, u32[]{:S(2)}, u32[]{:S(2)}) collective-permute-start(bf16[544,256]{1,0:T(8,128)(2,1)S(1)} %fusion.refs_1_), channel_id=1, source_target_pairs={{0,16},{1,17},{8,24},{9,25},{16,0},{17,1},{24,8},{25,9},{2,18},{3,... | collective-permute-start | bytes 835592 | tf_op jit(solution)/shard_map/ppermute | solution.py:194
  136.1 12.2 %collective-permute-start.8 = (bf16[544,256]{1,0:T(8,128)(2,1)S(1)}, bf16[544,256]{1,0:T(8,128)(2,1)S(1)}, u32[]{:S(2)}, u32[]{:S(2)}) collective-permute-start(bf16[544,256]{1,0:T(8,128)(2,1)S(1)} %collective-permute-done.7.refs_5_), channel_id=1, source_target_pairs={{0,16},{1,17},{8,24},{9,25},{16,0},{17,1},{24,8},{25,9},{2,18},{3,... | collective-permute-start | bytes 835592 | tf_op jit(solution)/shard_map/ppermute | solution.py:194
  137.2 11.2 %collective-permute-start.4 = (bf16[544,256]{1,0:T(8,128)(2,1)S(1)}, bf16[544,256]{1,0:T(8,128)(2,1)S(1)}, u32[]{:S(2)}, u32[]{:S(2)}) collective-permute-start(bf16[544,256]{1,0:T(8,128)(2,1)S(1)} %collective-permute-done.3.refs_6_), channel_id=1, source_target_pairs={{0,1},{1,0},{8,9},{9,8},{16,17},{17,16},{24,25},{25,24},{2,3},{3,2... | collective-permute-start | bytes 835592 | tf_op jit(solution)/shard_map/ppermute | solution.py:194
  138.3 10.5 %collective-permute-start.14 = (bf16[544,256]{1,0:T(8,128)(2,1)S(1)}, bf16[544,256]{1,0:T(8,128)(2,1)S(1)}, u32[]{:S(2)}, u32[]{:S(2)}) collective-permute-start(bf16[544,256]{1,0:T(8,128)(2,1)S(1)} %collective-permute-done.7.refs_5_), channel_id=1, source_target_pairs={{0,8},{1,9},{8,0},{9,1},{16,24},{17,25},{24,16},{25,17},{2,10},{3,... | collective-permute-start | bytes 835592 | tf_op jit(solution)/shard_map/ppermute | solution.py:194
  142.1 7.3 %collective-permute-start.15 = (bf16[544,256]{1,0:T(8,128)(2,1)S(1)}, bf16[544,256]{1,0:T(8,128)(2,1)S(1)}, u32[]{:S(2)}, u32[]{:S(2)}) collective-permute-start(bf16[544,256]{1,0:T(8,128)(2,1)S(1)} %collective-permute-done.3.refs_6_), channel_id=1, source_target_pairs={{0,8},{1,9},{8,0},{9,1},{16,24},{17,25},{24,16},{25,17},{2,10},{3,... | collective-permute-start | bytes 835592 | tf_op jit(solution)/shard_map/ppermute | solution.py:194
  148.3 2.4 collective-permute-start.17
  148.3 2.0 collective-permute-start.13
  148.8 1.8 collective-permute-start.16
  148.8 2.2 collective-permute-start.18
  161.2 17.1 %collective-permute-start.27 = (bf16[544,256]{1,0:T(8,128)(2,1)S(1)}, bf16[544,256]{1,0:T(8,128)(2,1)S(1)}, u32[]{:S(2)}, u32[]{:S(2)}) collective-permute-start(bf16[544,256]{1,0:T(8,128)(2,1)S(1)} %get-tuple-element.44), channel_id=1, source_target_pairs={{0,16},{1,17},{8,24},{9,25},{16,0},{17,1},{24,8},{25,9},{2,18},{3,... | collective-permute-start | bytes 835592 | tf_op jit(solution)/shard_map/ppermute | solution.py:194
  161.9 12.8 %collective-permute-start.19 = (bf16[544,256]{1,0:T(8,128)(2,1)S(1)}, bf16[544,256]{1,0:T(8,128)(2,1)S(1)}, u32[]{:S(2)}, u32[]{:S(2)}) collective-permute-start(bf16[544,256]{1,0:T(8,128)(2,1)S(1)} %get-tuple-element.44), channel_id=1, source_target_pairs={{0,1},{1,0},{8,9},{9,8},{16,17},{17,16},{24,25},{25,24},{2,3},{3,2... | collective-permute-start | bytes 835592 | tf_op jit(solution)/shard_map/ppermute | solution.py:194
  163.5 14.8 %collective-permute-start.26 = (bf16[544,256]{1,0:T(8,128)(2,1)S(1)}, bf16[544,256]{1,0:T(8,128)(2,1)S(1)}, u32[]{:S(2)}, u32[]{:S(2)}) collective-permute-start(bf16[544,256]{1,0:T(8,128)(2,1)S(1)} %get-tuple-element.45), channel_id=1, source_target_pairs={{0,1},{1,0},{8,9},{9,8},{16,17},{17,16},{24,25},{25,24},{2,3},{3,2... | collective-permute-start | bytes 835592 | tf_op jit(solution)/shard_map/ppermute | solution.py:194
  163.9 12.0 %collective-permute-start.20 = (bf16[544,256]{1,0:T(8,128)(2,1)S(1)}, bf16[544,256]{1,0:T(8,128)(2,1)S(1)}, u32[]{:S(2)}, u32[]{:S(2)}) collective-permute-start(bf16[544,256]{1,0:T(8,128)(2,1)S(1)} %get-tuple-element.45), channel_id=1, source_target_pairs={{0,16},{1,17},{8,24},{9,25},{16,0},{17,1},{24,8},{25,9},{2,18},{3,... | collective-permute-start | bytes 835592 | tf_op jit(solution)/shard_map/ppermute | solution.py:194
  165.3 21.2 %collective-permute-start.25 = (bf16[1088,256]{1,0:T(8,128)(2,1)S(1)}, bf16[1088,256]{1,0:T(8,128)(2,1)S(1)}, u32[]{:S(2)}, u32[]{:S(2)}) collective-permute-start(bf16[1088,256]{1,0:T(8,128)(2,1)S(1)} %get-tuple-element.59.refs_0_), channel_id=1, source_target_pairs={{0,8},{1,9},{8,0},{9,1},{16,24},{17,25},{24,16},{25,17},{2,10},{3,... | collective-permute-start | bytes 1671176 | tf_op jit(solution)/shard_map/ppermute | solution.py:194
  175.9 10.0 %collective-permute-start.21 = (bf16[544,256]{1,0:T(8,128)(2,1)S(1)}, bf16[544,256]{1,0:T(8,128)(2,1)S(1)}, u32[]{:S(2)}, u32[]{:S(2)}) collective-permute-start(bf16[544,256]{1,0:T(8,128)(2,1)S(1)} %collective-permute-done.20), channel_id=1, source_target_pairs={{0,1},{1,0},{8,9},{9,8},{16,17},{17,16},{24,25},{25,24},{2,3},{3,2... | collective-permute-start | bytes 835592 | tf_op jit(solution)/shard_map/ppermute | solution.py:194
  177.2 8.8 %collective-permute-start.22 = (bf16[544,256]{1,0:T(8,128)(2,1)S(1)}, bf16[544,256]{1,0:T(8,128)(2,1)S(1)}, u32[]{:S(2)}, u32[]{:S(2)}) collective-permute-start(bf16[544,256]{1,0:T(8,128)(2,1)S(1)} %collective-permute-done.19), channel_id=1, source_target_pairs={{0,16},{1,17},{8,24},{9,25},{16,0},{17,1},{24,8},{25,9},{2,18},{3,... | collective-permute-start | bytes 835592 | tf_op jit(solution)/shard_map/ppermute | solution.py:194
  178.4 8.2 %collective-permute-start.29 = (bf16[1088,256]{1,0:T(8,128)(2,1)S(1)}, bf16[1088,256]{1,0:T(8,128)(2,1)S(1)}, u32[]{:S(2)}, u32[]{:S(2)}) collective-permute-start(bf16[1088,256]{1,0:T(8,128)(2,1)S(1)} %constant_dynamic-update-slice_fusion.2.refs_3_), channel_id=1, source_target_pairs={{0,8},{1,9},{8,0},{9,1},{16,24},{17,25},{24,16},{25,17},{2,10},{3,... | collective-permute-start | bytes 1671176 | tf_op jit(solution)/shard_map/ppermute | solution.py:194
  178.4 8.1 %collective-permute-start.28 = (bf16[1088,256]{1,0:T(8,128)(2,1)S(1)}, bf16[1088,256]{1,0:T(8,128)(2,1)S(1)}, u32[]{:S(2)}, u32[]{:S(2)}) collective-permute-start(bf16[1088,256]{1,0:T(8,128)(2,1)S(1)} %constant_dynamic-update-slice_fusion.refs_2_), channel_id=1, source_target_pairs={{0,8},{1,9},{8,0},{9,1},{16,24},{17,25},{24,16},{25,17},{2,10},{3,... | collective-permute-start | bytes 1671176 | tf_op jit(solution)/shard_map/ppermute | solution.py:194
  185.9 1.8 collective-permute-start.23
  186.1 1.9 collective-permute-start.24
  194.5 30.3 %all-to-all-start.1 = ((bf16[32,128,128]{2,1,0:T(8,128)(2,1)}), bf16[32,128,128]{2,1,0:T(8,128)(2,1)S(1)}, u32[]{:S(2)}, u32[]{:S(2)}) async-start(bf16[32,128,128]{2,1,0:T(8,128)(2,1)} %get-tuple-element.64), calls=%async_computation.1 | async-start | bytes 2097152 | tf_op jit(solution)/shard_map/all_to_all | solution.py:824
